TPU v7x, 32 devices: a whole 2x2x4 slice. The times are simulated.
32 devices in a mesh: dp: 8 (over z, y), mp: 4 (over x, core).
Axes of the slice: x: 2, y: 2, z: 4, core: 2. Of those that a mesh axis runs over, the one named last changes fastest.
Arguments:
- byte_embeds: bfloat16 [4, 4096, 1024], P('mp', 'dp'), may hold values from -6 to 6
- lengths: int32 [4], replicated, may hold values from 3585 to 4096, as said below
- patch_in: bfloat16 [8388608], P(('dp', 'mp')), may hold values from -0.0625 to 0.0625
- mixer_in: bfloat16 [4489216], P(('dp', 'mp')), may hold values from -0.1875 to 0.1875
- mixer_out: bfloat16 [2097152], P(('dp', 'mp')), may hold values from -0.125 to 0.125
- patch_out: bfloat16 [8388608], P(('dp', 'mp')), may hold values from -0.1875 to 0.1875
- attend_in: bfloat16 [3145728], P(('dp', 'mp')), may hold values from -0.1875 to 0.1875
- attend_out: bfloat16 [1048576], P(('dp', 'mp')), may hold values from -0.375 to 0.375
- gate_weight: bfloat16 [1024, 4096], P('dp', 'mp'), may hold values from -0.1875 to 0.1875
- up_weight: bfloat16 [1024, 4096], P('dp', 'mp'), may hold values from -0.1875 to 0.1875
- down_weight: bfloat16 [4096, 1024], P('mp', 'dp'), may hold values from -0.09375 to 0.09375
- norm_global: float32 [1024], replicated, may hold values from 0.25 to 1.75
- conv_weight: float32 [4, 2304], replicated, may hold values from -3 to 3
- conv_bias: float32 [2304], replicated, may hold values from -3 to 3
- step_bias: float32 [32], replicated, may hold values from -1 to 1
- decay_rate: float32 [32], replicated, may hold values from -8 to -1
- skip_gain: float32 [32], replicated, may hold values from 0.5 to 1.5
- norm_gated: float32 [2048], replicated, may hold values from 0.25 to 1.75
- norm_attend: float32 [1024], replicated, may hold values from 0.25 to 1.75
- norm_feed: float32 [1024], replicated, may hold values from 0.25 to 1.75
- cotangent: bfloat16 [4, 4096, 1024], P('mp', 'dp'), may hold values from -6 to 6
Outputs:
- out_bytes: bfloat16 [4, 4096, 1024], P('mp', 'dp')
- grad_bytes: bfloat16 [4, 4096, 1024], P('mp', 'dp')
- grad_patch_in: float32 [8388608], P(('dp', 'mp'))
- grad_mixer_in: float32 [4489216], P(('dp', 'mp'))
- grad_mixer_out: float32 [2097152], P(('dp', 'mp'))
- grad_patch_out: float32 [8388608], P(('dp', 'mp'))
- grad_attend_in: float32 [3145728], P(('dp', 'mp'))
- grad_attend_out: float32 [1048576], P(('dp', 'mp'))
- grad_gate: float32 [1024, 4096], P('dp', 'mp')
- grad_up: float32 [1024, 4096], P('dp', 'mp')
- grad_down: float32 [4096, 1024], P('mp', 'dp')
- grad_norm_global: float32 [1024], replicated
- grad_conv_weight: float32 [4, 2304], replicated
- grad_conv_bias: float32 [2304], replicated
- grad_step_bias: float32 [32], replicated
- grad_decay_rate: float32 [32], replicated
- grad_skip_gain: float32 [32], replicated
- grad_norm_gated: float32 [2048], replicated
- grad_norm_attend: float32 [1024], replicated
- grad_norm_feed: float32 [1024], replicated
Inputs may be any that keep to these rules, and one draw needn't show every extreme that they name: `lengths`: every sequence uses more than its first (7) * 512 bytes; one sequence uses all 4096.
All inputs are finite; a program needn't handle non-finite values.
Results may differ from a plain program's by a relative error of at most 0.024.
Values may be sent and summed in bfloat16 or wider, within the bound.
A program may use at most 448 MiB of HBM per device.

v0:
```python
import functools

import jax
import jax.numpy as jnp
from jax import lax
from jax.experimental import pallas as pl
from jax.experimental.pallas import tpu as pltpu
from jax.sharding import PartitionSpec as P

D = 1024
PATCH = 8
INNER = 2048
HEADS_M = 32
STATE = 128
CONV = 4
HEADS_A = 16
HEAD_M = 64
HEAD_A = 64
PROJ = 4384
LANE = 128
VMEM_LIMIT = 60 * 2**20

HIGH = lax.Precision.HIGHEST
EPSILON = 1e-05
BF = jnp.bfloat16
F32 = jnp.float32


MESH = pl.DeviceIdType.MESH


def hail(axes, me, sizes):
    barrier = pltpu.get_barrier_semaphore()
    arrivals = 0
    for axis in axes:
        for k in range(1, sizes[axis]):
            pl.semaphore_signal(
                barrier,
                inc=1,
                device_id={axis: lax.rem(me[axis] + k, sizes[axis])},
                device_id_type=MESH,
            )
        arrivals += sizes[axis] - 1
    return arrivals


def greet(axes, me, sizes):
    pl.semaphore_wait(pltpu.get_barrier_semaphore(), hail(axes, me, sizes))


SUMS = ("sum", "sum1")
SPREADS = ("agh", "agh1")
DMA = pltpu.SemaphoreType.DMA


class Transfer:
    def __init__(self, kind, axis, size, source, target, sems, held=()):
        self.kind, self.axis, self.size = kind, axis, size
        self.source, self.target = source, target
        self.send, self.recv, self.local = sems
        self.here = lax.axis_index(axis)
        self.half = size // 2
        self.twin = self.here + 1 - 2 * lax.rem(self.here, 2)
        self.done, self.later, self.sent = [], [], []
        if kind in SUMS:
            self.mine, self.paired, self.loads = held

    def slot(self, peer):
        if callable(self.source):
            return self.source(peer)
        if self.kind in ("a2a", "sum"):
            return self.source.at[peer]
        if self.kind in ("a2a1", "sum1"):
            return self.source.at[:, peer]
        return self.source

    def block(self, peer):
        return self.target.at[:, peer] if self.kind == "agh1" else self.target.at[peer]

    def remote(self, source, target, number, peer):
        copy = pltpu.make_async_remote_copy(
            src_ref=source,
            dst_ref=target,
            send_sem=self.send.at[number],
            recv_sem=self.recv.at[number],
            device_id={self.axis: peer},
            device_id_type=MESH,
        )
        copy.start()
        return copy

    def start(self, keep_own=True):
        here, size, half, target = self.here, self.size, self.half, self.target
        if self.kind in SPREADS:
            for k in range(1, half):
                copy = self.remote(self.source, self.block(here), k, lax.rem(here + 2 * k, size))
                self.sent.append(copy)
                self.later.append((copy, k))
            self.done.append(self.remote(self.source, self.block(here), 0, self.twin))
        elif self.kind in SUMS:
            for k in list(range(1, half)) + [0]:
                owner = lax.rem(here + 2 * k, size)
                other = owner + 1 - 2 * lax.rem(here, 2)
                copy = self.remote(self.slot(other), self.paired.at[k], k, self.twin)
                self.sent.append(copy)
                load = None
                if self.loads is not None:
                    load = pltpu.make_async_copy(self.slot(owner), self.mine.at[k], self.loads.at[k])
                    load.start()
                self.later.append((copy, k, owner, load))
            return self
        else:
            for k in range(1, size):
                peer = lax.rem(here + k, size)
                self.done.append(self.remote(self.slot(peer), target.at[here], k - 1, peer))
        if keep_own:
            copy = pltpu.make_async_copy(self.slot(here), self.block(here), self.local)
            copy.start()
            self.done.append(copy)
        return self

    def relay(self):
        if self.kind in SPREADS:
            for copy, k in self.later:
                copy.wait_recv()
                block = self.block(lax.rem(self.here + self.size - 2 * k, self.size))
                self.done.append(self.remote(block, block, self.half - 1 + k, self.twin))
        elif self.kind in SUMS:
            for copy, k, owner, load in self.later:
                copy.wait_recv()
                if load is not None:
                    load.wait()
                    own = self.mine[k]
                else:
                    own = self.slot(owner)[...]
                self.mine[k] = (own.astype(F32) + self.paired[k].astype(F32)).astype(self.mine.dtype)
                if k:
                    self.done.append(
                        self.remote(self.mine.at[k], self.target.at[k], self.half - 1 + k, owner)
                    )
                elif load is not None:
                    own = pltpu.make_async_copy(self.mine.at[0], self.target.at[0], self.local)
                    own.start()
                    self.done.append(own)
        self.later = []
        return self

    def finish(self):
        for copy in self.done:
            copy.wait()
        for copy in self.sent:
            copy.wait_send()
        self.done, self.sent = [], []
        return self

    def total(self):
        self.relay()
        self.finish()
        summed = self.mine[0].astype(F32)
        for k in range(1, self.half):
            summed = summed + self.target[k].astype(F32)
        return summed


def transfer_sems(size):
    return [DMA((size - 1,)), DMA((size - 1,)), DMA]


def exchange_kernel(plan, sizes, *refs):
    count = len(plan)
    sources, targets = refs[:count], refs[count : 2 * count]
    scratch = list(refs[2 * count :])
    axes = sorted({axis for _, axis in plan})
    greet(axes, {axis: lax.axis_index(axis) for axis in axes}, sizes)
    moves = []
    for (kind, axis), source, target in zip(plan, sources, targets):
        sems = [scratch.pop(0) for _ in range(3)]
        held = [scratch.pop(0) for _ in range(3)] if kind in SUMS else ()
        moves.append(Transfer(kind, axis, sizes[axis], source, target, sems, held).start())
    order = lambda move: (move.kind not in SUMS, move.axis != "mp")
    for move in sorted(moves, key=order):
        move.relay()
    for move in moves:
        move.finish()


def exchange(ident, *steps):
    plan = tuple((kind, axis) for kind, axis, _ in steps)
    arrays = [array for _, _, array in steps]
    sizes = {axis: lax.axis_size(axis) for _, axis in plan}
    shapes = []
    scratch = []
    moved = 0
    for kind, axis, array in steps:
        shape = array.shape
        size = sizes[axis]
        if kind in ("ag", "agh"):
            shape = (size,) + shape
        elif kind == "agh1":
            shape = (shape[0], size) + shape[1:]
        elif kind == "a2a1":
            shape = (size, shape[0]) + shape[2:]
        elif kind == "sum":
            shape = (size // 2,) + shape[1:]
        elif kind == "sum1":
            shape = (size // 2, shape[0]) + shape[2:]
        shapes.append(jax.ShapeDtypeStruct(shape, array.dtype))
        moved += shapes[-1].size * array.dtype.itemsize
        scratch += transfer_sems(size)
        if kind in SUMS:
            scratch += [pltpu.VMEM(shape, array.dtype)] * 2 + [DMA((size // 2,))]
    return pl.pallas_call(
        functools.partial(exchange_kernel, plan, sizes),
        out_shape=shapes,
        in_specs=[pl.BlockSpec(memory_space=pl.ANY)] * len(plan),
        out_specs=[pl.BlockSpec(memory_space=pl.ANY)] * len(plan),
        scratch_shapes=scratch,
        compiler_params=pltpu.CompilerParams(
            collective_id=ident, has_side_effects=True, vmem_limit_bytes=VMEM_LIMIT
        ),
        cost_estimate=pl.CostEstimate(flops=0, bytes_accessed=64 * moved, transcendentals=0),
    )(*arrays)


def attend_forward_kernel(
    global_ref,
    w_out_ref,
    inputs_ref,
    gain_ref,
    feed_gain_ref,
    w_ref,
    local_ref,
    low_ref,
    qkv_ref,
    attended_ref,
    after_ref,
    feed_ref,
    probs_ref,
    leaving_ref,
    slots_ref,
    chunks_ref,
    *sems,
):
    rows = local_ref.shape[0]
    step = min(rows, 256)
    n_dp, patches, byte_cols = slots_ref.shape
    arrivals = hail(("dp",), {"dp": lax.axis_index("dp")}, {"dp": n_dp})
    leaving_ref[...] = product(global_ref[...], w_out_ref[...]).astype(BF).reshape(slots_ref.shape)
    pl.semaphore_wait(pltpu.get_barrier_semaphore(), arrivals)
    Transfer("a2a", "dp", n_dp, leaving_ref, slots_ref, sems).start().finish()
    for byte in range(PATCH):
        for chunk in range(D // LANE):
            column = byte * D + chunk * LANE
            there = slice(column % byte_cols, column % byte_cols + LANE)
            chunks_ref[chunk, pl.ds(byte, patches, stride=PATCH), :] = slots_ref[
                column // byte_cols, :, there
            ].astype(F32)
    mask = patch_mask(LANE)
    first = lax.broadcasted_iota(jnp.int32, (LANE, LANE), 1) < HEAD_A

    def some(index, _):
        at = pl.ds(pl.multiple_of(index * step, step), step)
        chunks = [chunks_ref[chunk, at, :] for chunk in range(D // LANE)]
        local = inputs_ref[at, :].astype(F32) + jnp.concatenate(chunks, axis=1)
        local_ref[at, :] = local
        low = root_norm(local, gain_ref[...]).astype(BF)
        low_ref[at, :] = low
        qkv_ref[at, :] = product(low, w_ref[:, : 3 * D]).astype(BF)

        def heads(inner, _):
            within = pl.ds(pl.multiple_of(index * step + inner * LANE, LANE), LANE)
            pairs = range(D // LANE)
            scores = []
            for pair in pairs:
                query = qkv_ref[within, pair * LANE : (pair + 1) * LANE]
                keyed = qkv_ref[within, D + pair * LANE : D + (pair + 1) * LANE]
                for half in (first, ~first):
                    scores.append(right_product(jnp.where(half, query, 0), keyed))
            probs = []
            for head, score in enumerate(scores):
                probs.append(patch_probs(score, mask).astype(BF))
                probs_ref[head, within, :] = probs[head]
            for pair in pairs:
                valued = qkv_ref[within, 2 * D + pair * LANE : 2 * D + (pair + 1) * LANE]
                attended_ref[within, pair * LANE : (pair + 1) * LANE] = jnp.where(
                    first, product(probs[2 * pair], valued), product(probs[2 * pair + 1], valued)
                ).astype(BF)
            return 0

        lax.fori_loop(0, step // LANE, heads, 0)
        after = local + product(attended_ref[at, :], w_ref[:, 3 * D :])
        after_ref[at, :] = after
        feed_ref[at, :] = root_norm(after, feed_gain_ref[...]).astype(BF)
        return 0

    lax.fori_loop(0, rows // step, some, 0)


def patch_mask(count):
    row = lax.broadcasted_iota(jnp.int32, (count, count), 0)
    column = lax.broadcasted_iota(jnp.int32, (count, count), 1)
    return (row // PATCH == column // PATCH) & (column <= row)


def patch_probs(scores, mask):
    scores = jnp.where(mask, scores * HEAD_A ** (-0.5), -1e30)
    expo = jnp.exp(scores - jnp.max(scores, axis=-1, keepdims=True))
    return expo / jnp.sum(expo, axis=-1, keepdims=True)


def attend_forward(ident, global_low, w_patch_out, inputs_low, norm_attend, norm_feed, w_attend):
    rows = inputs_low.shape[0]
    n_dp = lax.axis_size("dp")
    slots = (n_dp, rows // PATCH, w_patch_out.shape[1])
    return pl.pallas_call(
        attend_forward_kernel,
        out_shape=[
            jax.ShapeDtypeStruct((rows, D), F32),
            jax.ShapeDtypeStruct((rows, D), BF),
            jax.ShapeDtypeStruct((rows, 3 * D), BF),
            jax.ShapeDtypeStruct((rows, D), BF),
            jax.ShapeDtypeStruct((rows, D), F32),
            jax.ShapeDtypeStruct((rows, D), BF),
            jax.ShapeDtypeStruct((HEADS_A, rows, LANE), BF),
        ],
        in_specs=[pl.BlockSpec(memory_space=pltpu.VMEM)] * 6,
        out_specs=[pl.BlockSpec(memory_space=pltpu.VMEM)] * 7,
        scratch_shapes=[
            pltpu.VMEM(slots, BF),
            pltpu.VMEM(slots, BF),
            pltpu.VMEM((D // LANE, rows, LANE), F32),
        ]
        + transfer_sems(n_dp),
        compiler_params=pltpu.CompilerParams(
            collective_id=ident, has_side_effects=True, vmem_limit_bytes=VMEM_LIMIT
        ),
        cost_estimate=pl.CostEstimate(
            flops=2 * rows * D * 4 * D, bytes_accessed=24 * D * D, transcendentals=rows * 16 * LANE
        ),
    )(global_low, w_patch_out, inputs_low, norm_attend[None], norm_feed[None], w_attend)


def norm_back(values, gain, grad):
    scale = lax.rsqrt(jnp.mean(values * values, axis=-1, keepdims=True) + EPSILON)
    scaled = grad * gain
    along = jnp.mean(scaled * values, axis=-1, keepdims=True)
    return scale * scaled - values * (scale * scale * scale * along), grad * values * scale


def attend_backward_kernel(
    grad_feed_ref,
    grad_final_ref,
    local_ref,
    after_ref,
    low_ref,
    qkv_ref,
    attended_ref,
    probs_ref,
    gain_ref,
    feed_gain_ref,
    w_ref,
    grad_local_ref,
    grad_slots_ref,
    grad_w_ref,
    grad_more_ref,
    grad_gain_ref,
    grad_feed_gain_ref,
    grads_ref,
    chunks_ref,
    slots_ref,
    *sems,
):
    rows = local_ref.shape[0]
    step = min(rows, 256)
    n_dp, _, byte_cols = grad_slots_ref.shape
    arrivals = hail(("dp",), {"dp": lax.axis_index("dp")}, {"dp": n_dp})
    first = lax.broadcasted_iota(jnp.int32, (LANE, LANE), 1) < HEAD_A
    grad_gain_ref[...] = jnp.zeros_like(grad_gain_ref)
    grad_feed_gain_ref[...] = jnp.zeros_like(grad_feed_gain_ref)

    def some(index, _):
        at = pl.ds(pl.multiple_of(index * step, step), step)
        grad_after, gains = norm_back(after_ref[at, :], feed_gain_ref[...], grad_feed_ref[at, :])
        grad_feed_gain_ref[...] += jnp.sum(gains, axis=0, keepdims=True)
        grad_after = grad_after + grad_final_ref[at, :].astype(F32)
        grad_low = grad_after.astype(BF)
        grads_ref[at, 3 * D :] = grad_low
        grad_attended = right_product(grad_low, w_ref[:, 3 * D :]).astype(BF)
        grads_ref[at, :D] = grad_attended

        def heads(inner, _):
            within = pl.ds(pl.multiple_of(index * step + inner * LANE, LANE), LANE)
            pairs = range(D // LANE)

            def part(number, pair):
                return slice(number * D + pair * LANE, number * D + (pair + 1) * LANE)

            given = [grads_ref[within, part(0, pair)] for pair in pairs]
            grad_probs = []
            for pair in pairs:
                for half in (first, ~first):
                    grad_probs.append(
                        right_product(jnp.where(half, given[pair], 0), qkv_ref[within, part(2, pair)])
                    )
            grad_scores = []
            for head, grad in enumerate(grad_probs):
                probs = probs_ref[head, within, :].astype(F32)
                inside = jnp.sum(grad * probs, axis=-1, keepdims=True)
                grad_scores.append((probs * (grad - inside) * HEAD_A ** (-0.5)).astype(BF))
            for pair in pairs:
                query, keyed = qkv_ref[within, part(0, pair)], qkv_ref[within, part(1, pair)]
                two = (2 * pair, 2 * pair + 1)
                results = (
                    [product(grad_scores[head], keyed) for head in two],
                    [left_product(grad_scores[head], query) for head in two],
                    [left_product(probs_ref[head, within, :], given[pair]) for head in two],
                )
                for number in range(3):
                    grads_ref[within, part(number, pair)] = jnp.where(first, *results[number]).astype(BF)
            return 0

        lax.fori_loop(0, step // LANE, heads, 0)
        grad_normed = right_product(grads_ref[at, : 3 * D], w_ref[:, : 3 * D])
        grad_local, gains = norm_back(local_ref[at, :], gain_ref[...], grad_normed)
        grad_gain_ref[...] += jnp.sum(gains, axis=0, keepdims=True)
        grad_local = grad_after + grad_local
        grad_local_ref[at, :] = grad_local
        for chunk in range(D // LANE):
            chunks_ref[chunk, at, :] = grad_local[:, chunk * LANE : (chunk + 1) * LANE]
        return 0

    lax.fori_loop(0, rows // step, some, 0)
    for byte in range(PATCH):
        for chunk in range(D // LANE):
            slots_ref[byte, :, chunk * LANE : (chunk + 1) * LANE] = chunks_ref[
                chunk, pl.ds(byte, rows // PATCH, stride=PATCH), :
            ].astype(BF)
    shares = D // byte_cols

    def slot(peer):
        if shares == 1:
            return slots_ref.at[peer]
        column = pl.multiple_of(lax.rem(peer, shares) * byte_cols, byte_cols)
        return slots_ref.at[peer // shares, :, pl.ds(column, byte_cols)]

    pl.semaphore_wait(pltpu.get_barrier_semaphore(), arrivals)
    move = Transfer("a2a", "dp", n_dp, slot, grad_slots_ref, sems).start()

    n_mp, _, k_rows, _ = grad_w_ref.shape
    each = 256 // (n_mp * k_rows)

    def columns(index, _):
        at = pl.ds(pl.multiple_of(index * 256, 256), 256)
        for source, number, there in (
            (low_ref, 0, slice(0, 2 * D)),
            (low_ref, 2, slice(0, D)),
            (attended_ref, 3, slice(D, 2 * D)),
        ):
            width = there.stop - there.start
            target = grad_w_ref if number == 0 else grad_more_ref
            grad = left_product(source[:, at], grads_ref[:, number * D : number * D + width])
            grad = grad.astype(BF)
            for place in range(each):
                for owner in range(n_mp):
                    start = (place * n_mp + owner) * k_rows
                    target[owner, index * each + place, :, there] = grad[start : start + k_rows]
        return 0

    lax.fori_loop(0, D // 256, columns, 0)
    move.finish()


def attend_backward(ident, grad_feed, grad_final, local_in, after, low, qkv, attended, probs, gain, feed_gain, w):
    rows = local_in.shape[0]
    n_dp, n_mp = lax.axis_size("dp"), lax.axis_size("mp")
    vmem = pl.BlockSpec(memory_space=pltpu.VMEM)
    return pl.pallas_call(
        attend_backward_kernel,
        out_shape=[
            jax.ShapeDtypeStruct((rows, D), F32),
            jax.ShapeDtypeStruct((n_dp, rows // PATCH, PATCH * D // n_dp), BF),
            jax.ShapeDtypeStruct((n_mp, n_dp, D // (n_dp * n_mp), 2 * D), BF),
            jax.ShapeDtypeStruct((n_mp, n_dp, D // (n_dp * n_mp), 2 * D), BF),
            jax.ShapeDtypeStruct((1, D), F32),
            jax.ShapeDtypeStruct((1, D), F32),
        ],
        in_specs=[vmem] * 11,
        out_specs=[vmem, pl.BlockSpec(memory_space=pl.ANY)] + [vmem] * 4,
        scratch_shapes=[
            pltpu.VMEM((rows, 4 * D), BF),
            pltpu.VMEM((D // LANE, rows, LANE), F32),
            pltpu.VMEM((PATCH, rows // PATCH, D), BF),
        ]
        + transfer_sems(n_dp),
        compiler_params=pltpu.CompilerParams(
            collective_id=ident, has_side_effects=True, vmem_limit_bytes=VMEM_LIMIT
        ),
        cost_estimate=pl.CostEstimate(
            flops=4 * rows * D * 4 * D, bytes_accessed=40 * D * D, transcendentals=rows * 16 * LANE
        ),
    )(grad_feed, grad_final, local_in, after, low, qkv, attended, probs, gain[None], feed_gain[None], w)


def feed_kernel(
    n_mp,
    x_ref,
    c_ref,
    w_ref,
    out_ref,
    grad_feed_ref,
    grads_ref,
    held,
    hidden,
    grad_gate,
    grad_up,
    grad_held,
    paired,
    arrived,
    staged,
    own_sem,
    stage_sems,
    ag_send,
    ag_recv,
    pair_send,
    pair_recv,
    far_send,
    far_recv,
):
    rows = x_ref.shape[0]
    chips = n_mp // 2
    units = w_ref.shape[-1]
    here = lax.axis_index("mp")
    core = lax.rem(here, 2)
    twin = here + 1 - 2 * core
    pieces = 2
    size = rows // pieces
    greet(("mp",), {"mp": here}, {"mp": n_mp})

    def block(owner):
        return pl.ds(pl.multiple_of(owner * rows, rows), rows)

    def part(owner, piece):
        return pl.ds(pl.multiple_of(owner * rows + piece * size, size), size)

    def remote(source, target, send, recv, peer):
        copy = pltpu.make_async_remote_copy(
            src_ref=source,
            dst_ref=target,
            send_sem=send,
            recv_sem=recv,
            device_id={"mp": peer},
            device_id_type=MESH,
        )
        copy.start()
        return copy

    own = pltpu.make_async_copy(x_ref, held.at[block(here)], own_sem)
    own.start()
    far = [lax.rem(here + 2 * k, n_mp) for k in range(chips)]
    came = [lax.rem(here + n_mp - 2 * k, n_mp) for k in range(chips)]
    direct = {}
    near = remote(x_ref, held.at[block(here)], ag_send.at[0, 0], ag_recv.at[0, 0], twin)
    for piece in range(pieces):
        for k in range(1, chips):
            direct[k, piece] = remote(
                x_ref.at[part(0, piece)],
                held.at[part(here, piece)],
                ag_send.at[k, piece],
                ag_recv.at[k, piece],
                far[k],
            )

    def weight(number):
        return w_ref[:, number].reshape(D, units)

    stored, relays, pairs, sends = [], {}, {}, {}

    def work(owner, piece):
        number = len(stored)
        slot = number % 2
        if number >= 2:
            stored[number - 2].wait()
        at = part(owner, piece)
        x = held[at, :]
        gate = product(x, weight(0))
        up = product(x, weight(1))
        sigmoid = jax.nn.sigmoid(gate)
        silu = gate * sigmoid
        low = (silu * up).astype(BF)
        hidden[at, :] = low
        grad_hidden = product(c_ref[at, :], weight(2))
        gate_low = (grad_hidden * up * sigmoid * (1.0 + gate * (1.0 - sigmoid))).astype(BF)
        up_low = (grad_hidden * silu).astype(BF)
        grad_gate[at, :] = gate_low
        grad_up[at, :] = up_low
        staged[slot] = right_product(low, weight(2)).astype(BF)
        grad_held[at, :] = (
            right_product(gate_low, weight(0)) + right_product(up_low, weight(1))
        ).astype(BF)
        copy = pltpu.make_async_copy(staged.at[slot], out_ref.at[at], stage_sems.at[number])
        copy.start()
        stored.append(copy)

    def relay(k, piece):
        direct[k, piece].wait_recv()
        at = part(came[k], piece)
        relays[k, piece] = remote(
            held.at[at], held.at[at], ag_send.at[chips - 1 + k, piece], ag_recv.at[chips - 1 + k, piece], twin
        )

    def other(k):
        return came[k] + 1 - 2 * core

    def to_twin(k, piece):
        pairs[k, piece] = remote(
            grad_held.at[part(other(k), piece)],
            paired.at[k, part(0, piece)],
            pair_send.at[k, piece],
            pair_recv.at[k, piece],
            twin,
        )

    def onward(k, piece):
        pairs[k, piece].wait_recv()
        at = part(came[k], piece)
        both = grad_held[at, :].astype(F32) + paired[k, part(0, piece), :].astype(F32)
        grad_held[at, :] = both.astype(BF)
        if k:
            sends[k, piece] = remote(
                grad_held.at[at],
                arrived.at[k - 1, part(0, piece)],
                far_send.at[k - 1, piece],
                far_recv.at[k - 1, piece],
                came[k],
            )

    own.wait()
    for piece in range(pieces):
        work(here, piece)
    near.wait_recv()
    for piece in range(pieces):
        for k in range(1, chips):
            relay(k, piece)
        work(twin, piece)
        to_twin(0, piece)
        for k in range(1, chips):
            if piece:
                onward(k, piece - 1)
            relays[k, piece].wait_recv()
            work(other(k), piece)
            to_twin(k, piece)
            work(came[k], piece)

    def tiles(start, stop):
        def some(index, _):
            at = pl.ds(pl.multiple_of(index * LANE, LANE), LANE)
            x = held[:, at]
            each = grads_ref.shape[2]
            owners = pl.ds(index * (LANE // each), LANE // each)

            def store(number, value):
                grads_ref[owners, number] = value.astype(BF).reshape(LANE // each, each, units)

            store(0, left_product(x, grad_gate[...]))
            store(1, left_product(x, grad_up[...]))
            store(2, left_product(c_ref[:, at], hidden[...]))
            return 0

        lax.fori_loop(start, stop, some, 0)

    for k in range(1, chips):
        onward(k, pieces - 1)
    count = D // LANE
    tiles(0, count)
    for piece in range(pieces):
        onward(0, piece)
    total_here = grad_held[block(here), :].astype(F32)
    for k in range(1, chips):
        for piece in range(pieces):
            sends[k, piece].wait_recv()
        total_here = total_here + arrived[k - 1].astype(F32)
    grad_feed_ref[...] = total_here
    near.wait_send()
    for group in (direct, relays, pairs, sends):
        for copy in group.values():
            copy.wait_send()
    for copy in stored[-2:]:
        copy.wait()


def feed_section(ident, feed_low, grad_rows, weights):
    n_mp = lax.axis_size("mp")
    rows = feed_low.shape[0]
    every = rows * n_mp
    chips = n_mp // 2
    units = weights.shape[-1]
    dma = pltpu.SemaphoreType.DMA
    vmem = pl.BlockSpec(memory_space=pltpu.VMEM)
    return pl.pallas_call(
        functools.partial(feed_kernel, n_mp),
        out_shape=[
            jax.ShapeDtypeStruct((every, D), BF),
            jax.ShapeDtypeStruct((rows, D), F32),
            jax.ShapeDtypeStruct(weights.shape, BF),
        ],
        in_specs=[vmem] * 3,
        out_specs=[pl.BlockSpec(memory_space=pl.ANY), vmem, vmem],
        scratch_shapes=[
            pltpu.VMEM((every, D), BF),
            pltpu.VMEM((every, units), BF),
            pltpu.VMEM((every, units), BF),
            pltpu.VMEM((every, units), BF),
            pltpu.VMEM((every, D), BF),
            pltpu.VMEM((chips, rows, D), BF),
            pltpu.VMEM((chips - 1, rows, D), BF),
            pltpu.VMEM((2, rows // 2, D), BF),
            dma,
            dma((2 * n_mp,)),
            dma((n_mp - 1, 2)),
            dma((n_mp - 1, 2)),
            dma((chips, 2)),
            dma((chips, 2)),
            dma((chips - 1, 2)),
            dma((chips - 1, 2)),
        ],
        compiler_params=pltpu.CompilerParams(
            collective_id=ident, has_side_effects=True, vmem_limit_bytes=VMEM_LIMIT
        ),
        cost_estimate=pl.CostEstimate(
            flops=18 * every * D * units, bytes_accessed=30 * D * D, transcendentals=every * units
        ),
    )(feed_low, grad_rows, weights)


def product(left, right):
    return jnp.dot(left, right, preferred_element_type=F32)


def left_product(left, right):
    return lax.dot_general(left, right, (((0,), (0,)), ((), ())), preferred_element_type=F32)


def right_product(left, right):
    return lax.dot_general(left, right, (((1,), (1,)), ((), ())), preferred_element_type=F32)


def total(parts):
    return jnp.sum(parts.astype(F32), axis=0)


def root_norm(values, gain):
    return values * lax.rsqrt(jnp.mean(values * values, axis=-1, keepdims=True) + EPSILON) * gain


def shifted(values, steps):
    if steps == 0:
        return values
    row = lax.broadcasted_iota(jnp.int32, values.shape, 0)
    return jnp.where(row >= steps, pltpu.roll(values, steps, 0), 0.0)


def lifted(values, steps):
    if steps == 0:
        return values
    count = values.shape[0]
    row = lax.broadcasted_iota(jnp.int32, values.shape, 0)
    return jnp.where(row < count - steps, pltpu.roll(values, count - steps, 0), 0.0)


def running(values, move):
    steps = 1
    while steps < values.shape[0]:
        values = values + move(values, steps)
        steps *= 2
    return values


def softplus(values):
    return jnp.maximum(values, 0.0) + jnp.log1p(jnp.exp(-jnp.abs(values)))


class Mixer:
    def __init__(self, projected, inner, conv_weight, conv_bias, step_bias, decay_rate):
        self.inner = inner
        self.count = projected.shape[0]
        self.width = min(inner, LANE)
        self.per_group = self.width // HEAD_M
        self.tile = min(self.count, 256)
        edge = 2 * inner + 2 * STATE
        self.conv_input = projected[:, inner:edge]
        self.conv_weight = conv_weight
        summed = conv_bias + conv_weight[CONV - 1 : CONV] * self.conv_input
        for shift in range(1, CONV):
            row = CONV - 1 - shift
            summed = summed + conv_weight[row : row + 1] * shifted(self.conv_input, shift)
        self.sigmoid = jax.nn.sigmoid(summed)
        self.summed = summed
        self.activated = summed * self.sigmoid
        self.raw = projected[:, edge:] + step_bias
        self.step = softplus(self.raw)
        self.rate = jnp.exp(decay_rate)
        self.log_decay = running(self.step * -self.rate, shifted)
        self.log_decay_t = self.log_decay.T
        self.step_t = self.step.T
        low = self.activated.astype(BF)
        self.heads_low = low[:, :inner]
        self.input_low = low[:, inner : inner + STATE]
        self.output_low = low[:, inner + STATE :]
        lane = lax.broadcasted_iota(jnp.int32, (1, self.width), 1)
        self.lanes = [lane // HEAD_M == h for h in range(self.per_group)]

    def tiles(self):
        for start in range(0, self.count, self.tile):
            stop = start + self.tile
            scores = right_product(self.output_low[start:stop], self.input_low[:stop])
            row = lax.broadcasted_iota(jnp.int32, scores.shape, 0) + start
            causal = row >= lax.broadcasted_iota(jnp.int32, scores.shape, 1)
            yield start, stop, scores, causal

    def factor(self, head, start, stop, causal):
        spread = self.log_decay[start:stop, head : head + 1] - self.log_decay_t[head : head + 1, :stop]
        return jnp.exp(jnp.where(causal, spread, -1e30))

    def groups(self):
        return range(self.inner // self.width)

    def merged(self, parts):
        if len(parts) == 1:
            return parts[0]
        return jnp.where(self.lanes[0], parts[0], parts[1])


def mixer_forward_kernel(
    inner, normed_ref, w_ref, w_out_ref, conv_weight_ref, conv_bias_ref, step_bias_ref, decay_ref, skip_ref, gain_ref,
    projected_ref, values_ref, parts_ref, squares_ref,
):
    projected_ref[...] = product(normed_ref[...], w_ref[...])
    mixer = Mixer(
        projected_ref[...], inner, conv_weight_ref[...], conv_bias_ref[...], step_bias_ref[...], decay_ref[...]
    )
    for start, stop, scores, causal in mixer.tiles():
        for group in mixer.groups():
            at = slice(group * mixer.width, (group + 1) * mixer.width)
            parts = []
            for h in range(mixer.per_group):
                head = group * mixer.per_group + h
                weights = (
                    mixer.factor(head, start, stop, causal) * scores * mixer.step_t[head : head + 1, :stop]
                )
                parts.append(product(weights.astype(BF), mixer.heads_low[:stop, at]))
            values_ref[start:stop, at] = (
                mixer.merged(parts) + skip_ref[:, at] * mixer.activated[start:stop, at]
            )
    gate = projected_ref[:, :inner]
    gated = values_ref[...] * (gate * jax.nn.sigmoid(gate))
    squares_ref[...] = lax.dot_general(
        jnp.ones((8, inner), F32),
        gated * gated,
        (((1,), (1,)), ((), ())),
        precision=HIGH,
        preferred_element_type=F32,
    )
    parts_ref[...] = product((gated * gain_ref[...]).astype(BF), w_out_ref[...]).astype(BF)


def mixer_backward_kernel(
    inner,
    grad_ref,
    scales_ref,
    alongs_ref,
    normed_ref,
    projected_ref,
    values_ref,
    w_ref,
    w_out_ref,
    conv_weight_ref,
    conv_bias_ref,
    step_bias_ref,
    decay_ref,
    skip_ref,
    gain_ref,
    parts_ref,
    grad_w_ref,
    grad_w_out_ref,
    grad_conv_weight_ref,
    grad_conv_bias_ref,
    grad_heads_ref,
    grad_skip_ref,
    grad_gain_ref,
    grad_act_ref,
    columns_ref,
    grads_ref,
):
    mixer = Mixer(
        projected_ref[...], inner, conv_weight_ref[...], conv_bias_ref[...], step_bias_ref[...], decay_ref[...]
    )
    count = mixer.count
    edge = 2 * inner + 2 * STATE
    gate = projected_ref[:, :inner]
    sigmoid = jax.nn.sigmoid(gate)
    silu = gate * sigmoid
    values = values_ref[...]
    gated = values * silu
    scales = scales_ref[...]
    grad = grad_ref[...]
    grad_w_out_ref[...] = left_product((gated * scales * gain_ref[...]).astype(BF), grad).astype(BF)
    grad_mixed = right_product(grad, w_out_ref[...])
    grad_gain_ref[...] = jnp.sum(grad_mixed * gated * scales, axis=0, keepdims=True)
    grad_gated = scales * gain_ref[...] * grad_mixed - gated * (scales**3 * alongs_ref[...] / INNER)
    grad_values = grad_gated * silu
    grads_ref[:, :inner] = (grad_gated * values * (sigmoid * (1.0 + gate * (1.0 - sigmoid)))).astype(BF)
    heads_x = mixer.activated[:, :inner]
    grad_skip_ref[...] = jnp.sum(grad_values * heads_x, axis=0, keepdims=True)
    grad_act_ref[:, :inner] = grad_values * skip_ref[...]
    grad_act_ref[:, inner:] = jnp.zeros((count, 2 * STATE), F32)
    columns_ref[...] = jnp.zeros_like(columns_ref)
    grad_low = grad_values.astype(BF)
    lane = lax.broadcasted_iota(jnp.int32, (mixer.tile, LANE), 1)
    grad_decays = []
    for start, stop, scores, causal in mixer.tiles():
        grad_scores = jnp.zeros_like(scores)
        grad_decay = jnp.zeros((mixer.tile, LANE), F32)
        for group in mixer.groups():
            at = slice(group * mixer.width, (group + 1) * mixer.width)
            grad_group = grad_low[start:stop, at]
            parts = []
            for h in range(mixer.per_group):
                head = group * mixer.per_group + h
                row = slice(head, head + 1)
                factor = mixer.factor(head, start, stop, causal)
                step = mixer.step_t[row, :stop]
                unstepped = factor * scores
                grad_weights = right_product(
                    jnp.where(mixer.lanes[h], grad_group, 0), mixer.heads_low[:stop, at]
                )
                parts.append(left_product((unstepped * step).astype(BF), grad_group))
                grad_scores = grad_scores + grad_weights * factor * step
                grad_unstepped = grad_weights * unstepped
                columns_ref[row, :stop] += jnp.sum(grad_unstepped, axis=0, keepdims=True)
                summed = jnp.sum(grad_unstepped * step, axis=1, keepdims=True)
                grad_decay = jnp.where(lane == head, summed, grad_decay)
            grad_act_ref[:stop, at] += mixer.merged(parts)
        grad_decays.append(grad_decay)
        low = grad_scores.astype(BF)
        grad_act_ref[:stop, inner : inner + STATE] += left_product(low, mixer.output_low[start:stop])
        grad_act_ref[start:stop, inner + STATE :] += product(low, mixer.input_low[:stop])
    columns = columns_ref[...].T
    grad_decay = jnp.concatenate(grad_decays, axis=0) - mixer.step * columns
    onward = running(grad_decay, lifted)
    grad_step = columns - onward * mixer.rate
    grad_raw = grad_step * jax.nn.sigmoid(mixer.raw)
    grads_ref[:, edge:] = grad_raw.astype(BF)
    grad_heads_ref[0:1] = jnp.sum(grad_raw, axis=0, keepdims=True)
    grad_heads_ref[1:2] = -jnp.sum(onward * mixer.step, axis=0, keepdims=True) * mixer.rate
    grad_summed = grad_act_ref[...] * (mixer.sigmoid * (1.0 + mixer.summed * (1.0 - mixer.sigmoid)))
    grad_conv_bias_ref[...] = jnp.sum(grad_summed, axis=0, keepdims=True)
    grad_conv = jnp.zeros_like(grad_summed)
    for shift in range(CONV):
        row = slice(CONV - 1 - shift, CONV - shift)
        grad_conv = grad_conv + conv_weight_ref[row] * lifted(grad_summed, shift)
        grad_conv_weight_ref[row] = jnp.sum(
            grad_summed * shifted(mixer.conv_input, shift), axis=0, keepdims=True
        )
    grads_ref[:, inner:edge] = grad_conv.astype(BF)
    parts_ref[...] = right_product(grads_ref[...], w_ref[...]).astype(BF)
    grad_w_ref[...] = left_product(normed_ref[...], grads_ref[...]).astype(BF)


def whole_kernel(kernel, shapes, operands, scratch=(), flops=0):
    vmem = pl.BlockSpec(memory_space=pltpu.VMEM)
    moved = sum(x.size * x.dtype.itemsize for x in list(operands) + list(shapes))
    return pl.pallas_call(
        kernel,
        out_shape=shapes,
        in_specs=[vmem] * len(operands),
        out_specs=[vmem] * len(shapes),
        scratch_shapes=list(scratch),
        compiler_params=pltpu.CompilerParams(vmem_limit_bytes=VMEM_LIMIT),
        cost_estimate=pl.CostEstimate(flops=flops, bytes_accessed=3 * moved, transcendentals=0),
    )(*operands)


def own_columns(array, place, width):
    return lax.dynamic_slice_in_dim(array, place * width, width, axis=-1)


def tucked(row):
    return jnp.pad(row[:, None, :], ((0, 0), (0, 7), (0, -row.shape[1] % LANE)))


def body(
    byte_embeds,
    lengths,
    patch_in,
    mixer_in,
    mixer_out,
    patch_out,
    attend_in,
    attend_out,
    gate_weight,
    up_weight,
    down_weight,
    norm_global,
    conv_weight,
    conv_bias,
    step_bias,
    decay_rate,
    skip_gain,
    norm_gated,
    norm_attend,
    norm_feed,
    cotangent,
):
    n_dp, n_mp = lax.axis_size("dp"), lax.axis_size("mp")
    devices = n_dp * n_mp
    rows = byte_embeds.shape[1]
    patches = rows // PATCH
    count = patches * n_dp
    group = lax.axis_index("mp")
    place = lax.axis_index("dp")
    length = jnp.sum(jnp.where(jnp.arange(lengths.shape[0], dtype=jnp.int32) == group, lengths, 0))
    position = place * rows + jnp.arange(rows, dtype=jnp.int32)
    keep = (position < length).astype(F32)[:, None]
    inputs = byte_embeds[0].astype(F32) * keep

    heads = HEADS_M // n_dp
    inner = heads * HEAD_M
    byte_cols = PATCH * D // n_dp
    k_rows = D // devices
    step_pad = -heads % LANE
    cols = 2 * inner + 2 * STATE + heads + step_pad

    w_attend = lax.all_gather(
        jnp.concatenate([attend_in.reshape(k_rows, -1), attend_out.reshape(k_rows, -1)], axis=1),
        ("dp", "mp"),
        axis=0,
        tiled=True,
    )
    w_feed = lax.all_gather(jnp.stack([gate_weight, up_weight, down_weight.T]), "dp", axis=0)
    grad_final = (cotangent[0].astype(F32) * keep).astype(BF)

    mixer_rows = mixer_in.reshape(k_rows, PROJ)
    shared = mixer_rows[:, 2 * INNER : 2 * INNER + 2 * STATE]
    by_part = jnp.concatenate(
        [
            mixer_rows[:, :INNER].reshape(k_rows, n_dp, inner),
            mixer_rows[:, INNER : 2 * INNER].reshape(k_rows, n_dp, inner),
            jnp.broadcast_to(shared[:, None], (k_rows, n_dp, 2 * STATE)),
            mixer_rows[:, 2 * INNER + 2 * STATE :].reshape(k_rows, n_dp, heads),
            jnp.zeros((k_rows, n_dp, step_pad), BF),
        ],
        axis=2,
    ).transpose(1, 0, 2)
    out_by_part = patch_out.reshape(k_rows, n_dp, byte_cols).transpose(1, 0, 2)
    patch_rows = inputs.astype(BF).reshape(patches, n_dp, byte_cols).transpose(1, 0, 2)
    patch_rows, mixer_cols, w_patch_in, grad_feed_rows = exchange(
        0,
        ("a2a", "dp", patch_rows),
        ("a2a", "dp", by_part),
        ("agh", "mp", patch_in.reshape(-1, D)),
        ("agh", "mp", grad_final),
    )
    patch_rows = patch_rows.reshape(count, byte_cols)
    w_patch_in = w_patch_in.reshape(byte_cols, D)
    parts = product(patch_rows, w_patch_in).reshape(n_dp, patches, D)
    parts, mixer_cols = exchange(1, ("sum", "dp", parts), ("agh1", "mp", mixer_cols))
    w_mixer_in = mixer_cols.reshape(D, cols)
    global_in = total(parts)
    normed, out_cols, w_mixer_out = exchange(
        2,
        ("agh", "dp", root_norm(global_in, norm_global).astype(BF)),
        ("a2a", "dp", out_by_part),
        ("agh", "mp", mixer_out.reshape(-1, D)),
    )
    w_mixer_out = w_mixer_out.reshape(inner, D)
    normed = normed.reshape(count, D)

    def own_conv(array):
        return jnp.concatenate(
            [own_columns(array[..., :INNER], place, inner), array[..., INNER:]], axis=-1
        )

    def own_heads(array):
        return jnp.pad(own_columns(array, place, heads), (0, step_pad))[None]

    own_gain = own_columns(norm_gated, place, inner)[None]
    mixer_params = (
        own_conv(conv_weight),
        own_conv(conv_bias)[None],
        own_heads(step_bias),
        own_heads(decay_rate),
        jnp.repeat(own_columns(skip_gain, place, heads), HEAD_M)[None],
        own_gain,
    )
    projected, values, parts, squares = whole_kernel(
        functools.partial(mixer_forward_kernel, inner),
        [
            jax.ShapeDtypeStruct((count, cols), F32),
            jax.ShapeDtypeStruct((count, inner), F32),
            jax.ShapeDtypeStruct((count, D), BF),
            jax.ShapeDtypeStruct((8, count), F32),
        ],
        (normed, w_mixer_in, w_mixer_out) + mixer_params,
        flops=2 * count * D * (cols + inner),
    )
    squares = squares[0].reshape(n_dp, patches)
    parts, squares, out_cols = exchange(
        3,
        ("sum", "dp", parts.reshape(n_dp, patches, D)),
        ("a2a", "dp", tucked(squares)),
        ("agh1", "mp", out_cols),
    )
    scale = lax.rsqrt(total(squares)[0, :patches] / INNER + EPSILON)
    unscaled = total(parts)
    global_out = global_in + scale[:, None] * unscaled
    w_patch_out = out_cols.reshape(D, byte_cols)
    global_low, scales = exchange(
        4,
        ("agh", "dp", global_out.astype(BF)),
        ("agh", "dp", tucked(scale[None])[0]),
    )
    global_low = global_low.reshape(count, D)
    scales = scales[:, 0, :patches].reshape(count, 1)
    local_in, attend_low, qkv, attended_low, after_attend, feed_low, probs = attend_forward(
        5, global_low, w_patch_out, inputs.astype(BF), norm_attend, norm_feed, w_attend
    )
    feed_parts, grad_feed_normed, grad_feed = feed_section(
        12, feed_low, grad_feed_rows.reshape(-1, D), w_feed
    )
    units = grad_feed.shape[-1]
    grad_feed = lax.psum_scatter(
        grad_feed.reshape(3 * D, units), "dp", scatter_dimension=0, tiled=True
    ).astype(F32)
    grad_gate, grad_up, grad_down = grad_feed.reshape(3, D // n_dp, units)
    grad_down = grad_down.T
    grad_local, grad_slots, grad_attend, grad_more, grad_norm_attend, grad_norm_feed = attend_backward(
        6,
        grad_feed_normed,
        grad_final,
        local_in,
        after_attend,
        attend_low,
        qkv,
        attended_low,
        probs,
        norm_attend,
        norm_feed,
        w_attend,
    )
    grad_norm_attend, grad_norm_feed = grad_norm_attend[0], grad_norm_feed[0]

    def owners(grad):
        return grad.astype(BF).reshape(n_dp, n_mp, -1, grad.shape[-1])

    grad_slots = grad_slots.reshape(count, byte_cols)
    grad_patch_out = owners(left_product(global_low, grad_slots))
    parts = right_product(grad_slots, w_patch_out).astype(BF).reshape(n_dp, patches, D)
    parts, grad_patch_out, grad_attend = exchange(
        7, ("sum", "dp", parts), ("sum1", "mp", grad_patch_out), ("sum", "mp", grad_attend)
    )
    grad_global_out = total(parts)
    grad_mixer_low = grad_global_out.astype(BF)
    along = jnp.sum(grad_mixer_low.astype(F32) * unscaled, axis=1)
    grad_mixer_low, alongs, grad_patch_out, grad_more = exchange(
        8,
        ("agh", "dp", grad_mixer_low),
        ("agh", "dp", tucked(along[None])[0]),
        ("a2a", "dp", total(grad_patch_out).astype(BF)),
        ("sum", "mp", grad_more),
    )
    grad_mixer_low = grad_mixer_low.reshape(count, D)
    alongs = alongs[:, 0, :patches].reshape(count, 1)
    conv_cols = inner + 2 * STATE
    (
        parts,
        grad_mixer_in,
        grad_mixer_out,
        grad_conv_weight,
        grad_conv_bias,
        grad_heads,
        grad_skip,
        grad_norm_gated,
    ) = whole_kernel(
        functools.partial(mixer_backward_kernel, inner),
        [
            jax.ShapeDtypeStruct((count, D), BF),
            jax.ShapeDtypeStruct((D, cols), BF),
            jax.ShapeDtypeStruct((inner, D), BF),
            jax.ShapeDtypeStruct((CONV, conv_cols), F32),
            jax.ShapeDtypeStruct((1, conv_cols), F32),
            jax.ShapeDtypeStruct((2, heads + step_pad), F32),
            jax.ShapeDtypeStruct((1, inner), F32),
            jax.ShapeDtypeStruct((1, inner), F32),
        ],
        (grad_mixer_low, scales, alongs, normed, projected, values, w_mixer_in, w_mixer_out)
        + mixer_params,
        scratch=(
            pltpu.VMEM((count, conv_cols), F32),
            pltpu.VMEM((LANE, count), F32),
            pltpu.VMEM((count, cols), BF),
        ),
        flops=4 * count * D * (cols + inner),
    )
    grad_conv_bias, grad_norm_gated = grad_conv_bias[0], grad_norm_gated[0]
    grad_step_bias, grad_decay_rate = grad_heads[0, :heads], grad_heads[1, :heads]
    grad_skip_gain = jnp.sum(grad_skip.reshape(heads, HEAD_M), axis=1)
    parts = parts.reshape(n_dp, patches, D)
    grad_mixer_in = owners(grad_mixer_in)
    parts, grad_mixer_out, grad_mixer_in, feed_parts, grad_attend = exchange(
        9,
        ("sum", "dp", parts),
        ("sum", "mp", grad_mixer_out.reshape(n_mp, -1, D)),
        ("sum1", "mp", grad_mixer_in),
        ("sum", "mp", feed_parts.reshape(n_mp, rows, D)),
        ("sum", "dp", total(grad_attend).astype(BF)),
    )
    grad_mixer_out = total(grad_mixer_out).reshape(-1)
    _, pull_global = jax.vjp(root_norm, global_in, norm_global)
    grad_global_norm, grad_norm_global = pull_global(total(parts))
    grad_global_low = (grad_global_out + grad_global_norm).astype(BF)

    def all_columns(part, whole):
        return lax.dynamic_update_slice_in_dim(
            jnp.zeros(part.shape[:-1] + (whole,), F32), part, place * part.shape[-1], axis=-1
        )

    small = [
        grad_norm_global,
        jnp.concatenate(
            [all_columns(grad_conv_weight[:, :inner], INNER), grad_conv_weight[:, inner:]], axis=1
        ),
        jnp.concatenate([all_columns(grad_conv_bias[:inner], INNER), grad_conv_bias[inner:]]),
        all_columns(grad_step_bias, HEADS_M),
        all_columns(grad_decay_rate, HEADS_M),
        all_columns(grad_skip_gain, HEADS_M),
        all_columns(grad_norm_gated, INNER),
        grad_norm_attend,
        grad_norm_feed,
    ]
    packed = jnp.concatenate([part.reshape(-1) for part in small])
    packed = jnp.pad(packed, (0, -packed.shape[0] % (8 * LANE))).reshape(-1, LANE)
    grad_global_low, packed, grad_mixer_in, grad_more = exchange(
        10,
        ("agh", "dp", grad_global_low),
        ("agh", "mp", packed),
        ("a2a", "dp", total(grad_mixer_in).astype(BF)),
        ("sum", "dp", total(grad_more).astype(BF)),
    )
    grad_attend, grad_more = total(grad_attend), total(grad_more)
    grad_global_low = grad_global_low.reshape(count, D)
    grad_patch_rows = right_product(grad_global_low, w_patch_in).astype(BF)
    grad_patch_in = left_product(patch_rows, grad_global_low).astype(BF)
    grad_patch_rows, grad_patch_in, packed = exchange(
        11,
        ("a2a", "dp", grad_patch_rows.reshape(n_dp, patches, byte_cols)),
        ("sum", "mp", grad_patch_in.reshape(n_mp, -1, D)),
        ("agh", "dp", total(packed)),
    )
    grad_patch_in = total(grad_patch_in).reshape(-1)
    grad_patch_rows = grad_patch_rows.astype(F32).transpose(1, 0, 2).reshape(rows, D)
    grad_bytes = ((grad_local + grad_patch_rows) * keep).astype(BF)[None]
    out_bytes = ((after_attend + total(feed_parts)) * keep).astype(BF)[None]
    grad_patch_out = grad_patch_out.astype(F32).transpose(1, 0, 2).reshape(-1)
    grad_mixer_in = grad_mixer_in.astype(F32).transpose(1, 0, 2)
    edges = (inner, 2 * inner, 2 * inner + 2 * STATE, 2 * inner + 2 * STATE + heads)
    grad_mixer_in = jnp.concatenate(
        [
            grad_mixer_in[:, :, : edges[0]].reshape(k_rows, INNER),
            grad_mixer_in[:, :, edges[0] : edges[1]].reshape(k_rows, INNER),
            jnp.sum(grad_mixer_in[:, :, edges[1] : edges[2]], axis=1),
            grad_mixer_in[:, :, edges[2] : edges[3]].reshape(k_rows, HEADS_M),
        ],
        axis=1,
    ).reshape(-1)
    packed = total(packed).reshape(-1)
    summed, start = [], 0
    for part in small:
        summed.append(packed[start : start + part.size].reshape(part.shape))
        start += part.size
    return (
        out_bytes,
        grad_bytes,
        grad_patch_in,
        grad_mixer_in,
        grad_mixer_out,
        grad_patch_out,
        jnp.concatenate([grad_attend, grad_more[:, :D]], axis=1).reshape(-1),
        grad_more[:, D:].reshape(-1),
        grad_gate,
        grad_up,
        grad_down,
        *summed,
    )


def solution(mesh):
    flat = P(("dp", "mp"))
    split = P("mp", "dp", None)
    return jax.shard_map(
        body,
        mesh=mesh,
        in_specs=(split, P())
        + (flat,) * 6
        + (P("dp", "mp"), P("dp", "mp"), P("mp", "dp"))
        + (P(),) * 9
        + (split,),
        out_specs=(split, split)
        + (flat,) * 6
        + (P("dp", "mp"), P("dp", "mp"), P("mp", "dp"))
        + (P(),) * 9,
        check_vma=False,
    )
```

profile of v0, /device:TPU:0, one launch (start us, length us, event | category | flops | bytes accessed | tf_op | source)
XLA Modules:
  0.0 729.0 jit_solution(2807709630133978211)
XLA Ops:
  7.2 1.0 reshape.283
  8.3 0.9 reshape.284
  10.0 1.1 copy.96
  11.1 2.1 pad_maximum_fusion
  14.1 1.0 reshape.273.refs_2_
  15.3 1.1 copy.132
  18.1 1.3 dynamic_slice.23
  19.5 0.9 concatenate.24
  22.6 2.3 fusion.7.refs_0_
  24.9 1.7 fusion.1
  26.6 60.9 %shard_map.356 = (bf16[8,64,1024]{2,1,0:T(8,128)(2,1)}, bf16[8,32,896]{2,1,0:T(8,128)(2,1)}, bf16[4,256,1024]{2,1,0:T(8,128)(2,1)}, bf16[4,512,1024]{2,1,0:T(8,128)(2,1)}) custom-call(bf16[8,64,1024]{2,1,0:T(8,128)(2,1)} %fusion.7.refs_0_, bf16[8,32,896]{2,1,0:T(8,128)(2,1)} %bitcast.149, bf16[256,1024]{1,0:T(8,128)(2,1)} %reshape.273.refs_2_, ...), custom_call_target="tpu_custom_call" | custom-call | bytes 499122176 | tf_op jit(solution)/shard_map/pallas_call | solution.py:212
  87.5 4.6 fusion.22.refs_0_
  92.1 38.2 %shard_map.357 = (f32[4,64,1024]{2,1,0:T(8,128)}, bf16[8,4,32,896]{3,2,1,0:T(8,128)(2,1)}) custom-call(f32[8,64,1024]{2,1,0:T(8,128)} %fusion.22.refs_0_, bf16[8,32,896]{2,1,0:T(8,128)(2,1)} %get-tuple-element.83.refs_1_), custom_call_target="tpu_custom_call" | custom-call | bytes 184549376 | tf_op jit(solution)/shard_map/pallas_call | solution.py:212
  130.3 1.3 reduce_sum.232
  132.5 44.0 %shard_map.358 = (bf16[8,64,1024]{2,1,0:T(8,128)(2,1)}, bf16[8,32,1024]{2,1,0:T(8,128)(2,1)}, bf16[4,64,1024]{2,1,0:T(8,128)(2,1)}) custom-call(bf16[64,1024]{1,0:T(8,128)(2,1)} %multiply_convert_fusion.1.refs_0_, bf16[8,32,1024]{2,1,0:T(8,128)(2,1)} %bitcast.147, bf16[64,1024]{1,0:T(8,128)(2,1)} %reshape.276.refs_2_), custom_call_target="tpu_custom_call" | custom-call | bytes 134217728 | tf_op jit(solution)/shard_map/pallas_call | solution.py:212
  178.2 6.6 shard_map.359
  186.2 43.2 %shard_map.360 = (bf16[4,64,1024]{2,1,0:T(8,128)(2,1)}, f32[8,8,128]{2,1,0:T(8,128)}, bf16[8,4,32,1024]{3,2,1,0:T(8,128)(2,1)}) custom-call(bf16[8,64,1024]{2,1,0:T(8,128)(2,1)} %bitcast.154, f32[8,8,128]{2,1,0:T(8,128)} %pad.24.refs_1_, bf16[8,32,1024]{2,1,0:T(8,128)(2,1)} %get-tuple-element.90.refs_2_), custom_call_target="tpu_custom_call" | custom-call | bytes 169869312 | tf_op jit(solution)/shard_map/pallas_call | solution.py:212
  230.8 1.1 convert_reduce_fusion.6
  232.7 38.9 %shard_map.361 = (bf16[8,64,1024]{2,1,0:T(8,128)(2,1)}, f32[8,8,128]{2,1,0:T(8,128)}) custom-call(bf16[64,1024]{1,0:T(8,128)(2,1)} %add_convert_fusion.refs_0_, f32[8,128]{1,0:T(8,128)} %pad_bitcast_fusion.2.refs_1_), custom_call_target="tpu_custom_call" | custom-call | bytes 69206016 | tf_op jit(solution)/shard_map/pallas_call | solution.py:212
  271.6 34.9 %shard_map.362 = (f32[512,1024]{1,0:T(8,128)}, bf16[512,1024]{1,0:T(8,128)(2,1)}, bf16[512,3072]{1,0:T(8,128)(2,1)}, bf16[512,1024]{1,0:T(8,128)(2,1)}, f32[512,...) custom-call(bf16[512,1024]{1,0:T(8,128)(2,1)} %bitcast.193, bf16[1024,1024]{1,0:T(8,128)(2,1)} %bitcast.187, ...), custom_call_target="tpu_custom_call" | custom-call | flops 4294967296 | bytes 25165824 | tf_op jit(solution)/shard_map/pallas_call | solution.py:315
  306.6 71.6 %shard_map.363 = (bf16[2048,1024]{1,0:T(8,128)(2,1)}, f32[512,1024]{1,0:T(8,128)}, bf16[8,3,128,1024]{3,2,1,0:T(8,128)(2,1)}) custom-call(bf16[512,1024]{1,0:T(8,128)(2,1)} %get-tuple-element.96.x_ref, bf16[2048,1024]{1,0:T(8,128)(2,1)} %bitcast.184, bf16[8,3,128,1024]{3,2,1,0:T(8,128)(2,1)} %bitcast.183), custom_call_target="tpu_custom_call" | custom-call | flops 38654705664 | bytes 31457280 | tf_op jit(solution)/shard_map/pallas_call | solution.py:699
  379.1 0.9 reshape_squeeze.8.scales_ref
  380.0 57.4 %shard_map.364 = (f32[512,1024]{1,0:T(8,128)}, bf16[8,64,1024]{2,1,0:T(8,128)(2,1)}, bf16[4,8,32,2048]{3,2,1,0:T(8,128)(2,1)}, bf16[4,8,32,2048]{3,2,1,0:T(8,128...) custom-call(f32[512,1024]{1,0:T(8,128)} %get-tuple-element.98.grad_feed_ref, ...), custom_call_target="tpu_custom_call" | custom-call | flops 8589934592 | bytes 41943040 | tf_op jit(solution)/shard_map/pallas_call | solution.py:477
  437.4 3.7 convolution_convert_fusion.1
  441.1 2.7 bitcast_convert_fusion.1
  443.8 63.1 %shard_map.365 = (bf16[4,64,1024]{2,1,0:T(8,128)(2,1)}, bf16[2,8,32,1024]{3,2,1,0:T(8,128)(2,1)}, bf16[2,8,32,2048]{3,2,1,0:T(8,128)(2,1)}) custom-call(bf16[8,64,1024]{2,1,0:T(8,128)(2,1)} %bitcast.151, bf16[8,4,32,1024]{3,2,1,0:T(8,128)(2,1)} %bitcast.145, bf16[4,8,32,2048]{3,2,1,0:T(8,128)(2,1)} %get-tuple-element.105.refs_2_), custom_call_target="tpu_custom_call" | custom-call | bytes 234881024 | tf_op jit(solution)/shard_map/pallas_call | solution.py:212
  506.9 2.4 reduce_sum.238.refs_2_
  509.3 1.2 convert_reduce_fusion.5
  511.9 39.3 %shard_map.366 = (bf16[8,64,1024]{2,1,0:T(8,128)(2,1)}, f32[8,8,128]{2,1,0:T(8,128)}, bf16[8,32,1024]{2,1,0:T(8,128)(2,1)}, bf16[2,8,32,2048]{3,2,1,0:T(8,128)(2,1)}) custom-call(bf16[64,1024]{1,0:T(8,128)(2,1)} %get-tuple-element.225.refs_0_, f32[8,128]{1,0:T(8,128)} %pad_bitcast_fusion.1.refs_1_, bf16[8,32,1024]{2,1,0:T(8,128)(2,1)} %reduce_sum.238.refs_2_, ...), custom_call_target="tpu_custom_call" | custom-call | bytes 236978176 | tf_op jit(solution)/shard_map/pallas_call | solution.py:212
  551.9 0.9 reshape_squeeze.9.alongs_ref
  552.8 11.7 %shard_map.367 = (bf16[512,1024]{1,0:T(8,128)(2,1)}, bf16[1024,896]{1,0:T(8,128)(2,1)}, bf16[256,1024]{1,0:T(8,128)(2,1)}, f32[4,512]{1,0:T(4,128)}, f32[1,512]{...) custom-call(bf16[512,1024]{1,0:T(8,128)(2,1)} %bitcast.195, ...), custom_call_target="tpu_custom_call" | custom-call | flops 2415919104 | bytes 30763008 | tf_op jit(solution)/shard_map/pallas_call | solution.py:972
  565.4 1.9 reduce_sum.239.refs_4_
  568.5 45.5 %shard_map.368 = (bf16[4,64,1024]{2,1,0:T(8,128)(2,1)}, bf16[2,64,1024]{2,1,0:T(8,128)(2,1)}, bf16[2,8,32,896]{3,2,1,0:T(8,128)(2,1)}, bf16[2,512,1024]{2,1,0:T(8,128)(2,1)}, bf16[4,32,2048]{2,1,0:T(8,128)(2,1)}) custom-call(bf16[8,64,1024]{2,1,0:T(8,128)(2,1)} %bitcast.150, bf16[4,64,1024]{2,1,0:T(8,128)(2,1)} %bitcast.160, ...), custom_call_target="tpu_custom_call" | custom-call | bytes 276824064 | tf_op jit(solution)/shard_map/pallas_call | solution.py:212
  614.0 2.3 reduce_sum.245.refs_2_
  616.3 1.7 reduce_sum.246.refs_3_
  620.9 34.7 %shard_map.369 = (bf16[8,64,1024]{2,1,0:T(8,128)(2,1)}, f32[4,136,128]{2,1,0:T(8,128)}, bf16[8,32,896]{2,1,0:T(8,128)(2,1)}, bf16[4,32,2048]{2,1,0:T(8,128)(2,1)}) custom-call(bf16[64,1024]{1,0:T(8,128)(2,1)} %fusion.10.refs_0_, f32[136,128]{1,0:T(8,128)} %pad_bitcast_fusion.refs_1_, bf16[8,32,896]{2,1,0:T(8,128)(2,1)} %reduce_sum.245.refs_2_, ...), custom_call_target="tpu_custom_call" | custom-call | bytes 147849216 | tf_op jit(solution)/shard_map/pallas_call | solution.py:212
  655.6 1.2 convert_reduce_fusion.2
  658.2 1.3 reshape.306
  660.1 4.3 convolution_convert_fusion
  664.4 2.7 bitcast_convert_fusion
  667.1 36.9 %shard_map.370 = (bf16[8,64,1024]{2,1,0:T(8,128)(2,1)}, bf16[2,256,1024]{2,1,0:T(8,128)(2,1)}, f32[8,136,128]{2,1,0:T(8,128)}) custom-call(bf16[8,64,1024]{2,1,0:T(8,128)(2,1)} %bitcast.155, bf16[4,256,1024]{2,1,0:T(8,128)(2,1)} %bitcast.146, f32[136,128]{1,0:T(8,128)} %reduce_sum.247.refs_2_), custom_call_target="tpu_custom_call" | custom-call | bytes 169869312 | tf_op jit(solution)/shard_map/pallas_call | solution.py:212
  704.0 1.6 convert_reduce_fusion.1
  705.6 1.2 copy.114
  710.3 1.2 copy.116
  714.7 3.1 fusion.8
  717.8 1.5 copy.109
  720.3 1.0 copy.106
  721.3 1.0 copy.107
  (183 shorter events, 29.6 us)
Async XLA Ops:
  7.2 6.1 copy-start.15
  7.2 264.4 %all-gather.4.cloned.1.call-start = ((), (), s32[]{:S(2)}) async-start(), calls=%async_computation.1 | async-start | bytes 8650752 | tf_op jit(solution)/shard_map/all_gather | solution.py:1033
  9.9 4.2 copy-start.12
  9.9 296.7 %all-gather.6.cloned.1.call-start = ((), (), s32[]{:S(2)}) async-start(), calls=%async_computation.2 | async-start | bytes 7077888 | tf_op jit(solution)/shard_map/all_gather | solution.py:1039
  11.1 4.0 copy-start.13
  13.2 3.2 copy-start.18
  13.2 3.9 copy-start.29
  13.2 4.0 copy-start.30
  13.2 4.0 copy-start.31
  13.2 4.8 slice-start.2
  13.3 704.5 %reduce-scatter.4.cloned.1.call-start = ((), (), s32[]{:S(2)}) async-start(), calls=%async_computation.3 | async-start | bytes 7077888
  15.1 5.4 copy-start.32
  15.1 7.3 %copy-start = (bf16[1,512,1024]{2,1,0:T(8,128)(2,1)S(1)}, bf16[1,512,1024]{2,1,0:T(8,128)(2,1)}, u32[]{:S(2)}) copy-start(bf16[1,512,1024]{2,1,0:T(8,128)(2,1)} %param.21) | copy-start | bytes 3145732
  22.6 2.3 copy-start.7
  92.1 39.7 %copy-start.19 = (f32[1024]{0:T(1024)S(1)}, f32[1024]{0:T(1024)}, u32[]{:S(2)}) copy-start(f32[1024]{0:T(1024)} %param.32) | copy-start | bytes 12292
  92.1 84.9 %slice-start.3 = ((f32[2304]{0:T(1024)}), f32[256]{0:T(256)S(1)}, s32[]{:S(2)}) async-start(f32[2304]{0:T(1024)} %param.34), calls=%async_computation.7 | async-start | bytes 2048 | tf_op jit(solution)/shard_map/slice | solution.py:1080
  92.1 85.5 %slice-start = ((f32[4,2304]{1,0:T(4,128)}), f32[4,2048]{1,0:T(4,128)S(1)}, s32[]{:S(2)}) async-start(f32[4,2304]{1,0:T(4,128)} %param.33), calls=%async_computation.4 | async-start | bytes 65536 | tf_op jit(solution)/shard_map/slice | solution.py:1080
  92.1 85.5 %slice-start.1 = ((f32[4,2304]{1,0:T(4,128)}), f32[4,256]{1,0:T(4,128)S(1)}, s32[]{:S(2)}) async-start(f32[4,2304]{1,0:T(4,128)} %param.33), calls=%async_computation.5 | async-start | bytes 8192 | tf_op jit(solution)/shard_map/slice | solution.py:1080
  380.0 57.4 %copy-start.25 = (bf16[8,4,32,1024]{3,2,1,0:T(8,128)(2,1)S(1)}, bf16[8,4,32,1024]{3,2,1,0:T(8,128)(2,1)}, u32[]{:S(2)}) copy-start(bf16[8,4,32,1024]{3,2,1,0:T(8,128)(2,1)} %get-tuple-element.94) | copy-start | bytes 6291460
  437.4 3.7 copy-start.27
  437.4 3.7 copy-start.33
  552.8 12.5 %copy-start.3 = (bf16[2,8,32,2048]{3,2,1,0:T(8,128)(2,1)S(1)}, bf16[2,8,32,2048]{3,2,1,0:T(8,128)(2,1)}, u32[]{:S(2)}) copy-start(bf16[2,8,32,2048]{3,2,1,0:T(8,128)(2,1)} %get-tuple-element.118) | copy-start | bytes 6291460
  564.6 3.2 copy-start.24
  568.5 47.8 %copy-start.2 = (bf16[2,8,32,2048]{3,2,1,0:T(8,128)(2,1)S(1)}, bf16[2,8,32,2048]{3,2,1,0:T(8,128)(2,1)}, u32[]{:S(2)}) copy-start(bf16[2,8,32,2048]{3,2,1,0:T(8,128)(2,1)} %get-tuple-element.130) | copy-start | bytes 6291460
  614.0 4.0 copy-start.22
  614.0 4.2 copy-start.23
  614.0 4.9 copy-start.11
  616.3 2.8 copy-start.34
  616.3 3.0 copy-start.20
  616.3 3.0 copy-start.21
  619.0 37.8 %copy-start.10 = (bf16[4,32,2048]{2,1,0:T(8,128)(2,1)S(1)}, bf16[4,32,2048]{2,1,0:T(8,128)(2,1)}, u32[]{:S(2)}) copy-start(bf16[4,32,2048]{2,1,0:T(8,128)(2,1)} %get-tuple-element.138) | copy-start | bytes 1572868
  655.6 2.2 copy-start.14
  657.9 1.6 copy-start.16
  660.1 4.3 copy-start.26
  660.1 4.3 copy-start.28
  704.0 2.8 copy-start.8
  705.6 3.2 copy-start.17
  705.6 4.0 copy-start.9
  709.7 1.8 copy-start.1
  711.5 2.9 copy-start.6
  711.5 3.2 copy-start.5
  711.9 2.7 copy-start.4
Sparse Core Ops, SparseCore 0:
  11.5 116.3 all-gather.3
  130.7 141.3 all-gather.5
  378.4 172.7 reduce-scatter.3
where the time goes:
time: 734 us; the launch traced here: 729 us
  Pallas kernels  627 us (85%)
  other arithmetic  34.7 us (5%)
  local copies, waits for them, and re-layouts  34.6 us (5%)
  matrix products  17.9 us (2%)
  between operations  14.7 us (2%)
    pallas_call x10, Pallas kernels, exchange(): pl.pallas_call(functools.partial(exchange_kernel, plan, sizes), out_shape...  445 us
    pallas_call x1, Pallas kernels, feed_section(): pl.pallas_call(functools.partial(feed_kernel, n_mp), out_shape=[jax.Shape...  71.6 us
    pallas_call x1, Pallas kernels, attend_backward(): pl.pallas_call(attend_backward_kernel, out_shape=[jax.ShapeDtypeStruct((r...  57.4 us
    pallas_call x1, Pallas kernels, attend_forward(): pl.pallas_call(attend_forward_kernel, out_shape=[jax.ShapeDtypeStruct((ro...  34.9 us
    pallas_call x2, Pallas kernels, whole_kernel(): pl.pallas_call(kernel, out_shape=shapes, in_specs=[vmem] * len(operands),...  18.3 us
    reduce_sum x16, other arithmetic, total(): return jnp.sum(parts.astype(F32), axis=0)  16.7 us
  transfers between devices with their start and end apart: 3, of which 0 were waited for; matrix products, arithmetic and copies ran while one was open for 11% of the time, Pallas kernels for 76%

commit v1 on v0

--- a/solution.py
+++ b/solution.py
@@ -220,6 +220,165 @@
         ),
         cost_estimate=pl.CostEstimate(flops=0, bytes_accessed=64 * moved, transcendentals=0),
     )(*arrays)
+
+
+def chain_kernel(first, second, inner_steps, forwards, middle, counts, sizes, *refs):
+    refs = list(refs)
+
+    def take(count):
+        return [refs.pop(0) for _ in range(count)]
+
+    n_given, n_later, n_local, n_made = counts
+    sources, given, later = take(len(first)), take(n_given), take(n_later)
+    targets = {i: take(1)[0] for i in range(len(first)) if i not in inner_steps}
+    local, targets_second, targets_forward = take(n_local), take(len(second)), take(len(forwards))
+    axes = sorted({step[1] for step in first + second})
+    greet(axes, {axis: lax.axis_index(axis) for axis in axes}, sizes)
+
+    def transfer(kind, axis, source, target):
+        sems = take(3)
+        held = take(3) if kind in SUMS else ()
+        return Transfer(kind, axis, sizes[axis], source, target, sems, held)
+
+    moves = []
+    for index, (kind, axis) in enumerate(first):
+        target = take(1)[0] if index in inner_steps else targets[index]
+        moves.append(transfer(kind, axis, sources[index], target).start())
+    made = take(n_made)
+    more = []
+    for (kind, axis, source), target in zip(second, targets_second):
+        source = made[source] if source >= 0 else later[-1 - source]
+        more.append(transfer(kind, axis, source, target))
+    passed = []
+    for target in targets_forward:
+        buffer = take(1)[0]
+        passed.append((buffer, transfer("a2a", "dp", buffer, target)))
+    for move in moves:
+        if move.kind in SUMS:
+            move.relay()
+    extras = [index for index in inner_steps if index and index not in forwards]
+    for index in extras:
+        moves[index].finish()
+    results, kept = middle(moves[0].total(), *[moves[index].target for index in extras], *given)
+    for ref, value in zip(made, results):
+        ref[...] = value
+    for move in more:
+        move.start()
+    for ref, value in zip(local, kept):
+        ref[...] = value
+    for index, (buffer, move) in zip(forwards, passed):
+        buffer[...] = moves[index].total().astype(BF)
+        move.start()
+    for move in more:
+        if move.kind in SUMS:
+            move.relay()
+    for move in moves + more:
+        move.relay()
+    for move in moves + more + [move for _, move in passed]:
+        move.finish()
+
+
+def moved_shape(kind, size, shape):
+    if kind in ("ag", "agh"):
+        return (size,) + shape
+    if kind == "agh1":
+        return (shape[0], size) + shape[1:]
+    if kind == "a2a1":
+        return (size, shape[0]) + shape[2:]
+    if kind == "sum":
+        return (size // 2,) + shape[1:]
+    if kind == "sum1":
+        return (size // 2, shape[0]) + shape[2:]
+    return shape
+
+
+def chain(ident, first, middle, given, made, local, second, extras=(), forwards=()):
+    sizes = {axis: lax.axis_size(axis) for axis in ("dp", "mp")}
+    inner_steps = tuple(sorted({0} | set(extras) | set(forwards)))
+    later = [source for _, _, source in second if not isinstance(source, int)]
+    plan_second, seen = [], 0
+    shapes, local_shapes, second_shapes, scratch = [], list(local), [], []
+
+    def held(kind, axis, shape, dtype):
+        scratch.extend(transfer_sems(sizes[axis]))
+        if kind in SUMS:
+            scratch.extend([pltpu.VMEM(shape, dtype)] * 2 + [DMA((sizes[axis] // 2,))])
+
+    moved = 0
+    for index, (kind, axis, array) in enumerate(first):
+        shape = moved_shape(kind, sizes[axis], array.shape)
+        moved += 2 * array.size
+        if index in inner_steps:
+            scratch.append(pltpu.VMEM(shape, array.dtype))
+        else:
+            shapes.append(jax.ShapeDtypeStruct(shape, array.dtype))
+        held(kind, axis, shape, array.dtype)
+    scratch.extend(pltpu.VMEM(item.shape, item.dtype) for item in made)
+    for kind, axis, source in second:
+        item = source
+        if isinstance(source, int):
+            item = made[source]
+            plan_second.append((kind, axis, source))
+        else:
+            seen += 1
+            plan_second.append((kind, axis, -seen))
+        shape = moved_shape(kind, sizes[axis], item.shape)
+        second_shapes.append(jax.ShapeDtypeStruct(shape, item.dtype))
+        held(kind, axis, shape, item.dtype)
+    forward_shapes = []
+    for index in forwards:
+        kind, axis, array = first[index]
+        shape = moved_shape(kind, sizes[axis], array.shape)[1:]
+        forward_shapes.append(jax.ShapeDtypeStruct(shape, BF))
+        scratch.append(pltpu.VMEM(shape, BF))
+        held("a2a", "dp", shape, BF)
+    hbm, vmem = pl.BlockSpec(memory_space=pl.ANY), pl.BlockSpec(memory_space=pltpu.VMEM)
+    return pl.pallas_call(
+        functools.partial(
+            chain_kernel,
+            tuple((kind, axis) for kind, axis, _ in first),
+            tuple(plan_second),
+            inner_steps,
+            tuple(forwards),
+            middle,
+            (len(given), len(later), len(local), len(made)),
+            sizes,
+        ),
+        out_shape=shapes + local_shapes + second_shapes + forward_shapes,
+        in_specs=[hbm] * len(first) + [vmem] * len(given) + [hbm] * len(later),
+        out_specs=[hbm] * len(shapes)
+        + [vmem] * len(local_shapes)
+        + [hbm] * (len(second_shapes) + len(forward_shapes)),
+        scratch_shapes=scratch,
+        compiler_params=pltpu.CompilerParams(
+            collective_id=ident, has_side_effects=True, vmem_limit_bytes=VMEM_LIMIT
+        ),
+        cost_estimate=pl.CostEstimate(flops=0, bytes_accessed=64 * moved, transcendentals=0),
+    )(*[array for _, _, array in first], *given, *later)
+
+
+def norm_step(summed, gain_ref):
+    return [root_norm(summed, gain_ref[...]).astype(BF)], [summed]
+
+
+def mixed_step(summed, squares_ref, global_in_ref):
+    squares = squares_ref[0]
+    for index in range(1, squares_ref.shape[0]):
+        squares = squares + squares_ref[index]
+    scale = lax.rsqrt(squares / INNER + EPSILON)
+    return [(global_in_ref[...] + scale[:, :1] * summed).astype(BF), scale], [summed]
+
+
+def grad_mixed_step(summed, unscaled_ref):
+    low = summed.astype(BF)
+    along = jnp.sum(low.astype(F32) * unscaled_ref[...], axis=1, keepdims=True)
+    return [low, jnp.broadcast_to(along, (along.shape[0], LANE))], [summed]
+
+
+def grad_norm_step(summed, global_in_ref, gain_ref, grad_out_ref):
+    grad, gains = norm_back(global_in_ref[...], gain_ref[...], summed)
+    gains = jnp.sum(gains, axis=0, keepdims=True)
+    return [(grad_out_ref[...] + grad).astype(BF), jnp.broadcast_to(gains, (8, D))], []
 
 
 def attend_forward_kernel(
@@ -853,13 +1012,8 @@
             )
     gate = projected_ref[:, :inner]
     gated = values_ref[...] * (gate * jax.nn.sigmoid(gate))
-    squares_ref[...] = lax.dot_general(
-        jnp.ones((8, inner), F32),
-        gated * gated,
-        (((1,), (1,)), ((), ())),
-        precision=HIGH,
-        preferred_element_type=F32,
-    )
+    squares = jnp.sum(gated * gated, axis=1, keepdims=True)
+    squares_ref[...] = jnp.broadcast_to(squares, squares_ref.shape)
     parts_ref[...] = product((gated * gain_ref[...]).astype(BF), w_out_ref[...]).astype(BF)
 
 
@@ -901,12 +1055,12 @@
     silu = gate * sigmoid
     values = values_ref[...]
     gated = values * silu
-    scales = scales_ref[...]
+    scales = scales_ref[:, :1]
     grad = grad_ref[...]
     grad_w_out_ref[...] = left_product((gated * scales * gain_ref[...]).astype(BF), grad).astype(BF)
     grad_mixed = right_product(grad, w_out_ref[...])
     grad_gain_ref[...] = jnp.sum(grad_mixed * gated * scales, axis=0, keepdims=True)
-    grad_gated = scales * gain_ref[...] * grad_mixed - gated * (scales**3 * alongs_ref[...] / INNER)
+    grad_gated = scales * gain_ref[...] * grad_mixed - gated * (scales**3 * alongs_ref[:, :1] / INNER)
     grad_values = grad_gated * silu
     grads_ref[:, :inner] = (grad_gated * values * (sigmoid * (1.0 + gate * (1.0 - sigmoid)))).astype(BF)
     heads_x = mixer.activated[:, :inner]
@@ -1053,25 +1207,27 @@
     ).transpose(1, 0, 2)
     out_by_part = patch_out.reshape(k_rows, n_dp, byte_cols).transpose(1, 0, 2)
     patch_rows = inputs.astype(BF).reshape(patches, n_dp, byte_cols).transpose(1, 0, 2)
-    patch_rows, mixer_cols, w_patch_in, grad_feed_rows = exchange(
+    patch_rows, mixer_cols, w_patch_in = exchange(
         0,
         ("a2a", "dp", patch_rows),
         ("a2a", "dp", by_part),
         ("agh", "mp", patch_in.reshape(-1, D)),
-        ("agh", "mp", grad_final),
     )
     patch_rows = patch_rows.reshape(count, byte_cols)
     w_patch_in = w_patch_in.reshape(byte_cols, D)
     parts = product(patch_rows, w_patch_in).reshape(n_dp, patches, D)
-    parts, mixer_cols = exchange(1, ("sum", "dp", parts), ("agh1", "mp", mixer_cols))
+    row, lanes = jax.ShapeDtypeStruct((patches, D), F32), jax.ShapeDtypeStruct((patches, LANE), F32)
+    row_low = jax.ShapeDtypeStruct((patches, D), BF)
+    mixer_cols, global_in, normed, out_cols, w_mixer_out = chain(
+        1,
+        [("sum", "dp", parts), ("agh1", "mp", mixer_cols)],
+        norm_step,
+        [norm_global[None]],
+        [row_low],
+        [row],
+        [("agh", "dp", 0), ("a2a", "dp", out_by_part), ("agh", "mp", mixer_out.reshape(-1, D))],
+    )
     w_mixer_in = mixer_cols.reshape(D, cols)
-    global_in = total(parts)
-    normed, out_cols, w_mixer_out = exchange(
-        2,
-        ("agh", "dp", root_norm(global_in, norm_global).astype(BF)),
-        ("a2a", "dp", out_by_part),
-        ("agh", "mp", mixer_out.reshape(-1, D)),
-    )
     w_mixer_out = w_mixer_out.reshape(inner, D)
     normed = normed.reshape(count, D)
 
@@ -1098,29 +1254,30 @@
             jax.ShapeDtypeStruct((count, cols), F32),
             jax.ShapeDtypeStruct((count, inner), F32),
             jax.ShapeDtypeStruct((count, D), BF),
-            jax.ShapeDtypeStruct((8, count), F32),
+            jax.ShapeDtypeStruct((count, LANE), F32),
         ],
         (normed, w_mixer_in, w_mixer_out) + mixer_params,
         flops=2 * count * D * (cols + inner),
     )
-    squares = squares[0].reshape(n_dp, patches)
-    parts, squares, out_cols = exchange(
+    out_cols, grad_feed_rows, unscaled, global_low, scales = chain(
         3,
-        ("sum", "dp", parts.reshape(n_dp, patches, D)),
-        ("a2a", "dp", tucked(squares)),
-        ("agh1", "mp", out_cols),
-    )
-    scale = lax.rsqrt(total(squares)[0, :patches] / INNER + EPSILON)
-    unscaled = total(parts)
-    global_out = global_in + scale[:, None] * unscaled
+        [
+            ("sum", "dp", parts.reshape(n_dp, patches, D)),
+            ("a2a", "dp", squares.reshape(n_dp, patches, LANE)),
+            ("agh1", "mp", out_cols),
+            ("agh", "mp", grad_final),
+        ],
+        mixed_step,
+        [global_in],
+        [row_low, lanes],
+        [row],
+        [("agh", "dp", 0), ("agh", "dp", 1)],
+        extras=(1,),
+    )
     w_patch_out = out_cols.reshape(D, byte_cols)
-    global_low, scales = exchange(
-        4,
-        ("agh", "dp", global_out.astype(BF)),
-        ("agh", "dp", tucked(scale[None])[0]),
-    )
     global_low = global_low.reshape(count, D)
-    scales = scales[:, 0, :patches].reshape(count, 1)
+    scales = scales.reshape(count, LANE)
+
     local_in, attend_low, qkv, attended_low, after_attend, feed_low, probs = attend_forward(
         5, global_low, w_patch_out, inputs.astype(BF), norm_attend, norm_feed, w_attend
     )
@@ -1155,21 +1312,18 @@
     grad_slots = grad_slots.reshape(count, byte_cols)
     grad_patch_out = owners(left_product(global_low, grad_slots))
     parts = right_product(grad_slots, w_patch_out).astype(BF).reshape(n_dp, patches, D)
-    parts, grad_patch_out, grad_attend = exchange(
-        7, ("sum", "dp", parts), ("sum1", "mp", grad_patch_out), ("sum", "mp", grad_attend)
-    )
-    grad_global_out = total(parts)
-    grad_mixer_low = grad_global_out.astype(BF)
-    along = jnp.sum(grad_mixer_low.astype(F32) * unscaled, axis=1)
-    grad_mixer_low, alongs, grad_patch_out, grad_more = exchange(
-        8,
-        ("agh", "dp", grad_mixer_low),
-        ("agh", "dp", tucked(along[None])[0]),
-        ("a2a", "dp", total(grad_patch_out).astype(BF)),
-        ("sum", "mp", grad_more),
+    grad_attend, grad_global_out, grad_mixer_low, alongs, grad_more, grad_patch_out = chain(
+        7,
+        [("sum", "dp", parts), ("sum1", "mp", grad_patch_out), ("sum", "mp", grad_attend)],
+        grad_mixed_step,
+        [unscaled],
+        [row_low, lanes],
+        [row],
+        [("agh", "dp", 0), ("agh", "dp", 1), ("sum", "mp", grad_more)],
+        forwards=(1,),
     )
     grad_mixer_low = grad_mixer_low.reshape(count, D)
-    alongs = alongs[:, 0, :patches].reshape(count, 1)
+    alongs = alongs.reshape(count, LANE)
     conv_cols = inner + 2 * STATE
     (
         parts,
@@ -1206,26 +1360,12 @@
     grad_skip_gain = jnp.sum(grad_skip.reshape(heads, HEAD_M), axis=1)
     parts = parts.reshape(n_dp, patches, D)
     grad_mixer_in = owners(grad_mixer_in)
-    parts, grad_mixer_out, grad_mixer_in, feed_parts, grad_attend = exchange(
-        9,
-        ("sum", "dp", parts),
-        ("sum", "mp", grad_mixer_out.reshape(n_mp, -1, D)),
-        ("sum1", "mp", grad_mixer_in),
-        ("sum", "mp", feed_parts.reshape(n_mp, rows, D)),
-        ("sum", "dp", total(grad_attend).astype(BF)),
-    )
-    grad_mixer_out = total(grad_mixer_out).reshape(-1)
-    _, pull_global = jax.vjp(root_norm, global_in, norm_global)
-    grad_global_norm, grad_norm_global = pull_global(total(parts))
-    grad_global_low = (grad_global_out + grad_global_norm).astype(BF)
-
     def all_columns(part, whole):
         return lax.dynamic_update_slice_in_dim(
             jnp.zeros(part.shape[:-1] + (whole,), F32), part, place * part.shape[-1], axis=-1
         )
 
     small = [
-        grad_norm_global,
         jnp.concatenate(
             [all_columns(grad_conv_weight[:, :inner], INNER), grad_conv_weight[:, inner:]], axis=1
         ),
@@ -1239,22 +1379,34 @@
     ]
     packed = jnp.concatenate([part.reshape(-1) for part in small])
     packed = jnp.pad(packed, (0, -packed.shape[0] % (8 * LANE))).reshape(-1, LANE)
-    grad_global_low, packed, grad_mixer_in, grad_more = exchange(
-        10,
-        ("agh", "dp", grad_global_low),
-        ("agh", "mp", packed),
-        ("a2a", "dp", total(grad_mixer_in).astype(BF)),
-        ("sum", "dp", total(grad_more).astype(BF)),
-    )
+    grad_mixer_out, feed_parts, grad_attend, packed, grad_global_low, gains, grad_more, grad_mixer_in = chain(
+        9,
+        [
+            ("sum", "dp", parts),
+            ("sum1", "mp", grad_mixer_in),
+            ("sum", "mp", grad_mixer_out.reshape(n_mp, -1, D)),
+            ("sum", "mp", feed_parts.reshape(n_mp, rows, D)),
+            ("sum", "dp", total(grad_attend).astype(BF)),
+            ("agh", "mp", packed),
+        ],
+        grad_norm_step,
+        [global_in, norm_global[None], grad_global_out],
+        [row_low, jax.ShapeDtypeStruct((8, D), F32)],
+        [],
+        [("agh", "dp", 0), ("agh", "mp", 1), ("sum", "dp", total(grad_more).astype(BF))],
+        forwards=(1,),
+    )
+    grad_mixer_out = total(grad_mixer_out).reshape(-1)
     grad_attend, grad_more = total(grad_attend), total(grad_more)
     grad_global_low = grad_global_low.reshape(count, D)
     grad_patch_rows = right_product(grad_global_low, w_patch_in).astype(BF)
     grad_patch_in = left_product(patch_rows, grad_global_low).astype(BF)
-    grad_patch_rows, grad_patch_in, packed = exchange(
+    grad_patch_rows, grad_patch_in, packed, gains = exchange(
         11,
         ("a2a", "dp", grad_patch_rows.reshape(n_dp, patches, byte_cols)),
         ("sum", "mp", grad_patch_in.reshape(n_mp, -1, D)),
         ("agh", "dp", total(packed)),
+        ("agh", "dp", total(gains)),
     )
     grad_patch_in = total(grad_patch_in).reshape(-1)
     grad_patch_rows = grad_patch_rows.astype(F32).transpose(1, 0, 2).reshape(rows, D)
@@ -1289,6 +1441,7 @@
         grad_gate,
         grad_up,
         grad_down,
+        total(gains)[0],
         *summed,
     )
 

time: 734 us -> 707 us (0.963)
  Pallas kernels: 627 us -> 614 us
  other arithmetic: 34.7 us -> 26.1 us
    pallas_call x10 -> x2, Pallas kernels: 445 us -> 91.2 us  [exchange(): pl.pallas_call(functools.partial(exchange_kernel, plan, sizes), out_shape...]
    pallas_call x0 -> x4, Pallas kernels: none -> 342 us  [chain(): pl.pallas_call(functools.partial(chain_kernel, tuple(((kind, axis) for ki...]
    pallas_call x1, Pallas kernels: 71.6 us -> 61.7 us  [feed_section(): pl.pallas_call(functools.partial(feed_kernel, n_mp), out_shape=[jax.Shape...]
    pallas_call x1, Pallas kernels: 34.9 us -> 43.8 us  [attend_forward(): pl.pallas_call(attend_forward_kernel, out_shape=[jax.ShapeDtypeStruct((ro...]
    reduce_sum x16 -> x11, other arithmetic: 16.7 us -> 10.7 us  [total(): return jnp.sum(parts.astype(F32), axis=0)]
  transfers between devices with their start and end apart: 3 -> 3, of which waited for: 0 -> 0; matrix products, arithmetic and copies ran while one was open for 11% -> 9% of each run, Pallas kernels for 76% -> 79%
where the time goes in v1:
time: 707 us; the launch traced here: 702 us
  Pallas kernels  614 us (87%)
  local copies, waits for them, and re-layouts  28.8 us (4%)
  other arithmetic  26.1 us (4%)
  matrix products  17.5 us (2%)
  between operations  14.8 us (2%)
    pallas_call x4, Pallas kernels, chain(): pl.pallas_call(functools.partial(chain_kernel, tuple(((kind, axis) for ki...  342 us
    pallas_call x2, Pallas kernels, exchange(): pl.pallas_call(functools.partial(exchange_kernel, plan, sizes), out_shape...  91.2 us
    pallas_call x1, Pallas kernels, feed_section(): pl.pallas_call(functools.partial(feed_kernel, n_mp), out_shape=[jax.Shape...  61.7 us
    pallas_call x1, Pallas kernels, attend_backward(): pl.pallas_call(attend_backward_kernel, out_shape=[jax.ShapeDtypeStruct((r...  57.7 us
    pallas_call x1, Pallas kernels, attend_forward(): pl.pallas_call(attend_forward_kernel, out_shape=[jax.ShapeDtypeStruct((ro...  43.8 us
    pallas_call x2, Pallas kernels, whole_kernel(): pl.pallas_call(kernel, out_shape=shapes, in_specs=[vmem] * len(operands),...  17.8 us
  transfers between devices with their start and end apart: 3, of which 0 were waited for; matrix products, arithmetic and copies ran while one was open for 9% of the time, Pallas kernels for 79%

profile of v1, /device:TPU:0, one launch (start us, length us, event | category | flops | bytes accessed | tf_op | source)
XLA Modules:
  0.0 701.8 jit_solution(3048003629689334148)
XLA Ops:
  7.2 1.0 reshape.239
  8.3 0.9 reshape.240
  9.2 0.7 pad_maximum_fusion.2
  10.0 1.1 copy.92
  11.1 2.1 pad_maximum_fusion
  14.1 1.0 reshape.228.refs_2_
  15.3 1.1 copy.126
  16.4 0.7 reshape.231.refs_4_
  18.1 1.3 dynamic_slice.23
  19.5 0.9 concatenate.24
  22.0 2.3 fusion.7.refs_0_
  24.2 50.8 %shard_map.356 = (bf16[8,64,1024]{2,1,0:T(8,128)(2,1)}, bf16[8,32,896]{2,1,0:T(8,128)(2,1)}, bf16[4,256,1024]{2,1,0:T(8,128)(2,1)}) custom-call(bf16[8,64,1024]{2,1,0:T(8,128)(2,1)} %fusion.7.refs_0_, bf16[8,32,896]{2,1,0:T(8,128)(2,1)} %bitcast.143, bf16[256,1024]{1,0:T(8,128)(2,1)} %reshape.228.refs_2_), custom_call_target="tpu_custom_call" | custom-call | bytes 230686720 | tf_op jit(solution)/shard_map/pallas_call | solution.py:212
  75.0 4.6 fusion.17.refs_0_
  79.6 88.9 %shard_map.357 = (bf16[8,4,32,896]{3,2,1,0:T(8,128)(2,1)}, f32[64,1024]{1,0:T(8,128)}, bf16[8,64,1024]{2,1,0:T(8,128)(2,1)}, bf16[8,32,1024]{2,1,0:T(8,128)(2,1)}, bf16[4,64,1024]{2,1,0:T(8,128)(2,1)}) custom-call(f32[8,64,1024]{2,1,0:T(8,128)} %fusion.17.refs_0_, bf16[8,32,896]{2,1,0:T(8,128)(2,1)} %get-tuple-element.81.refs_1_, f32[1,1024]{1,0:T(1,128)} %bitcast.168, ...), custom_call_target="tpu_custom_call" | custom-call | bytes 96468992 | tf_op jit(solution)/shard_map/pallas_call | solution.py:336
  170.9 6.2 shard_map.358
  177.1 1.7 fusion.1
  178.8 84.4 %shard_map.359 = (bf16[8,4,32,1024]{3,2,1,0:T(8,128)(2,1)}, bf16[4,512,1024]{2,1,0:T(8,128)(2,1)}, f32[64,1024]{1,0:T(8,128)}, bf16[8,64,1024]{2,1,0:T(8,128)(2,1)}, f32[8,64,128]{2,1,0:T(8,128)}) custom-call(bf16[8,64,1024]{2,1,0:T(8,128)(2,1)} %bitcast.145, f32[8,64,128]{2,1,0:T(8,128)} %bitcast.161, bf16[8,32,1024]{2,1,0:T(8,128)(2,1)} %get-tuple-element.87.refs_2_, ...), custom_call_target="tpu_custom_call" | custom-call | bytes 176160768 | tf_op jit(solution)/shard_map/pallas_call | solution.py:336
  263.3 43.8 %shard_map.360 = (f32[512,1024]{1,0:T(8,128)}, bf16[512,1024]{1,0:T(8,128)(2,1)}, bf16[512,3072]{1,0:T(8,128)(2,1)}, bf16[512,1024]{1,0:T(8,128)(2,1)}, f32[512,...) custom-call(bf16[512,1024]{1,0:T(8,128)(2,1)} %bitcast.190, bf16[1024,1024]{1,0:T(8,128)(2,1)} %bitcast.184, ...), custom_call_target="tpu_custom_call" | custom-call | flops 4294967296 | bytes 25165824 | tf_op jit(solution)/shard_map/pallas_call | solution.py:474
  307.1 61.7 %shard_map.361 = (bf16[2048,1024]{1,0:T(8,128)(2,1)}, f32[512,1024]{1,0:T(8,128)}, bf16[8,3,128,1024]{3,2,1,0:T(8,128)(2,1)}) custom-call(bf16[512,1024]{1,0:T(8,128)(2,1)} %get-tuple-element.92.x_ref, bf16[2048,1024]{1,0:T(8,128)(2,1)} %bitcast.181, bf16[8,3,128,1024]{3,2,1,0:T(8,128)(2,1)} %bitcast.180), custom_call_target="tpu_custom_call" | custom-call | flops 38654705664 | bytes 31457280 | tf_op jit(solution)/shard_map/pallas_call | solution.py:858
  368.8 57.7 %shard_map.362 = (f32[512,1024]{1,0:T(8,128)}, bf16[8,64,1024]{2,1,0:T(8,128)(2,1)}, bf16[4,8,32,2048]{3,2,1,0:T(8,128)(2,1)}, bf16[4,8,32,2048]{3,2,1,0:T(8,128...) custom-call(f32[512,1024]{1,0:T(8,128)} %get-tuple-element.94.grad_feed_ref, ...), custom_call_target="tpu_custom_call" | custom-call | flops 8589934592 | bytes 41943040 | tf_op jit(solution)/shard_map/pallas_call | solution.py:636
  426.5 3.7 convolution_convert_fusion.1
  430.2 2.6 bitcast_convert_fusion.1
  432.8 103.8 %shard_map.363 = (bf16[2,8,32,2048]{3,2,1,0:T(8,128)(2,1)}, f32[64,1024]{1,0:T(8,128)}, bf16[8,64,1024]{2,1,0:T(8,128)(2,1)}, f32[8,64,128]{2,1,0:T(8,128)}, bf1...) custom-call(bf16[8,64,1024]{2,1,0:T(8,128)(2,1)} %bitcast.146, bf16[8,4,32,1024]{3,2,1,0:T(8,128)(2,1)} %bitcast.141, ...), custom_call_target="tpu_custom_call" | custom-call | bytes 469762048 | tf_op jit(solution)/shard_map/pallas_call | solution.py:336
  536.7 11.6 %shard_map.364 = (bf16[512,1024]{1,0:T(8,128)(2,1)}, bf16[1024,896]{1,0:T(8,128)(2,1)}, bf16[256,1024]{1,0:T(8,128)(2,1)}, f32[4,512]{1,0:T(4,128)}, f32[1,512]{...) custom-call(bf16[512,1024]{1,0:T(8,128)(2,1)} %bitcast.192, f32[512,128]{1,0:T(8,128)} %bitcast.195, ...), custom_call_target="tpu_custom_call" | custom-call | flops 2415919104 | bytes 32323584 | tf_op jit(solution)/shard_map/pallas_call | solution.py:1126
  548.4 0.9 slice_dynamic-update-slice_fusion
  549.8 1.3 reduce.5
  551.2 3.3 reduce_sum.133.refs_4_
  554.5 1.7 reduce_sum.135.refs_9_
  558.0 65.2 %shard_map.365 = (bf16[2,64,1024]{2,1,0:T(8,128)(2,1)}, bf16[2,512,1024]{2,1,0:T(8,128)(2,1)}, bf16[4,32,2048]{2,1,0:T(8,128)(2,1)}, f32[4,128,128]{2,1,0:T(8,12...) custom-call(bf16[8,64,1024]{2,1,0:T(8,128)(2,1)} %bitcast.144, ...), custom_call_target="tpu_custom_call" | custom-call | bytes 555745280 | tf_op jit(solution)/shard_map/pallas_call | solution.py:336
  623.2 1.2 convert_reduce_fusion.2
  624.4 1.1 convert_reduce_fusion.3
  625.6 0.8 copy.111
  626.9 1.3 reshape.264
  629.5 3.9 convolution_convert_fusion
  633.4 2.6 bitcast_convert_fusion
  636.1 40.4 %shard_map.366 = (bf16[8,64,1024]{2,1,0:T(8,128)(2,1)}, bf16[2,256,1024]{2,1,0:T(8,128)(2,1)}, f32[8,128,128]{2,1,0:T(8,128)}, f32[8,8,1024]{2,1,0:T(8,128)}) custom-call(bf16[8,64,1024]{2,1,0:T(8,128)(2,1)} %bitcast.147, bf16[4,256,1024]{2,1,0:T(8,128)(2,1)} %bitcast.140, f32[128,128]{1,0:T(8,128)} %reduce_sum.137.refs_2_, f32[8,1024]{1,0:T(8,128)} %reduce_sum.138.refs_3_), custom_call_target="tpu_custom_call" | custom-call | bytes 184549376 | tf_op jit(solution)/shard_map/pallas_call | solution.py:212
  676.4 1.6 convert_reduce_fusion.1
  678.1 1.2 copy.108
  679.9 0.7 slice.148
  681.2 0.7 copy.112
  681.9 0.8 copy.109
  683.4 1.2 copy.110
  685.7 0.7 fusion.14
  687.2 3.1 fusion.8
  690.4 1.5 copy.103
  692.0 0.8 slice_bitcast_fusion
  692.9 1.0 copy.100
  693.9 1.0 copy.101
  (150 shorter events, 14.5 us)
Async XLA Ops:
  7.2 6.1 copy-start.12
  7.2 256.0 %all-gather.4.cloned.1.call-start = ((), (), s32[]{:S(2)}) async-start(), calls=%async_computation.1 | async-start | bytes 8650752 | tf_op jit(solution)/shard_map/all_gather | solution.py:1187
  9.9 4.2 copy-start.8
  9.9 297.1 %all-gather.6.cloned.1.call-start = ((), (), s32[]{:S(2)}) async-start(), calls=%async_computation.2 | async-start | bytes 7077888 | tf_op jit(solution)/shard_map/all_gather | solution.py:1193
  11.1 4.0 copy-start.9
  13.2 3.2 copy-start.17
  13.2 3.9 copy-start.26
  13.2 4.0 copy-start.27
  13.2 4.0 copy-start.28
  13.2 4.8 slice-start.2
  13.3 677.1 %reduce-scatter.4.cloned.1.call-start = ((), (), s32[]{:S(2)}) async-start(), calls=%async_computation.3 | async-start | bytes 7077888
  15.1 5.4 copy-start.29
  15.1 6.6 copy-start
  79.6 90.1 %slice-start.3 = ((f32[2304]{0:T(1024)}), f32[256]{0:T(256)S(1)}, s32[]{:S(2)}) async-start(f32[2304]{0:T(1024)} %param.34), calls=%async_computation.7 | async-start | bytes 2048 | tf_op jit(solution)/shard_map/slice | solution.py:1236
  79.6 90.7 %slice-start = ((f32[4,2304]{1,0:T(4,128)}), f32[4,2048]{1,0:T(4,128)S(1)}, s32[]{:S(2)}) async-start(f32[4,2304]{1,0:T(4,128)} %param.33), calls=%async_computation.4 | async-start | bytes 65536 | tf_op jit(solution)/shard_map/slice | solution.py:1236
  79.6 90.7 %slice-start.1 = ((f32[4,2304]{1,0:T(4,128)}), f32[4,256]{1,0:T(4,128)S(1)}, s32[]{:S(2)}) async-start(f32[4,2304]{1,0:T(4,128)} %param.33), calls=%async_computation.5 | async-start | bytes 8192 | tf_op jit(solution)/shard_map/slice | solution.py:1236
  170.9 6.2 copy-start.6
  368.8 57.7 %copy-start.22 = (bf16[8,4,32,1024]{3,2,1,0:T(8,128)(2,1)S(1)}, bf16[8,4,32,1024]{3,2,1,0:T(8,128)(2,1)}, u32[]{:S(2)}) copy-start(bf16[8,4,32,1024]{3,2,1,0:T(8,128)(2,1)} %get-tuple-element.90) | copy-start | bytes 6291460
  426.5 3.7 copy-start.24
  426.5 3.7 copy-start.30
  548.3 6.2 copy-start.2
  554.5 1.7 copy-start.20
  554.5 2.0 copy-start.21
  554.5 2.6 copy-start.31
  554.5 2.8 copy-start.18
  554.5 2.8 copy-start.19
  623.2 3.2 copy-start.11
  626.6 1.6 copy-start.13
  626.6 2.2 copy-start.16
  626.6 2.9 copy-start.25
  629.5 3.9 copy-start.23
  676.4 2.8 copy-start.10
  676.4 4.1 copy-start.14
  678.0 3.8 copy-start.15
  678.0 4.6 copy-start.7
  682.8 1.8 copy-start.1
  684.6 2.3 copy-start.5
  684.6 2.6 copy-start.4
  685.0 2.2 copy-start.3
Sparse Core Ops, SparseCore 0:
  11.5 120.0 all-gather.3
  134.3 139.8 all-gather.5
  368.9 163.2 reduce-scatter.3

commit v2 on v1

--- a/solution.py
+++ b/solution.py
@@ -355,6 +355,64 @@
         ),
         cost_estimate=pl.CostEstimate(flops=0, bytes_accessed=64 * moved, transcendentals=0),
     )(*[array for _, _, array in first], *given, *later)
+
+
+def patch_in_kernel(
+    sizes, grad_ref, w_ref, rows_ref, packed_ref, gains_ref, out_rows_ref, grad_w_ref, out_packed_ref, out_gains_ref,
+    leaving, grads, mine, paired, came, *sems,
+):
+    axes = ("dp", "mp")
+    arrivals = hail(axes, {axis: lax.axis_index(axis) for axis in axes}, sizes)
+    leaving[...] = right_product(grad_ref[...], w_ref[...]).astype(BF).reshape(leaving.shape)
+    pl.semaphore_wait(pltpu.get_barrier_semaphore(), arrivals)
+    moves = [
+        Transfer("a2a", "dp", sizes["dp"], leaving, out_rows_ref, sems[:3]).start(),
+        Transfer("agh", "dp", sizes["dp"], packed_ref, out_packed_ref, sems[3:6]).start(),
+        Transfer("agh", "dp", sizes["dp"], gains_ref, out_gains_ref, sems[6:9]).start(),
+    ]
+    grads[...] = left_product(rows_ref[...], grad_ref[...]).astype(BF).reshape(grads.shape)
+    added = Transfer("sum", "mp", sizes["mp"], grads, came, sems[9:], (mine, paired, None)).start()
+    added.relay()
+    for move in moves:
+        move.relay()
+    grad_w_ref[...] = added.total()
+    for move in moves:
+        move.finish()
+
+
+def patch_in_backward(ident, grad, w, patch_rows, packed, gains, patches):
+    sizes = {axis: lax.axis_size(axis) for axis in ("dp", "mp")}
+    byte_cols = w.shape[0]
+    slots = (sizes["dp"], patches, byte_cols)
+    share = (byte_cols // sizes["mp"], D)
+    half = (sizes["mp"] // 2,) + share
+    hbm, vmem = pl.BlockSpec(memory_space=pl.ANY), pl.BlockSpec(memory_space=pltpu.VMEM)
+    return pl.pallas_call(
+        functools.partial(patch_in_kernel, sizes),
+        out_shape=[
+            jax.ShapeDtypeStruct(slots, BF),
+            jax.ShapeDtypeStruct(share, F32),
+            jax.ShapeDtypeStruct((sizes["dp"],) + packed.shape, F32),
+            jax.ShapeDtypeStruct((sizes["dp"],) + gains.shape, F32),
+        ],
+        in_specs=[vmem] * 3 + [hbm] * 2,
+        out_specs=[hbm, vmem, hbm, hbm],
+        scratch_shapes=[
+            pltpu.VMEM(slots, BF),
+            pltpu.VMEM((sizes["mp"],) + share, BF),
+            pltpu.VMEM(half, BF),
+            pltpu.VMEM(half, BF),
+            pltpu.VMEM(half, BF),
+        ]
+        + transfer_sems(sizes["dp"]) * 3
+        + transfer_sems(sizes["mp"]),
+        compiler_params=pltpu.CompilerParams(
+            collective_id=ident, has_side_effects=True, vmem_limit_bytes=VMEM_LIMIT
+        ),
+        cost_estimate=pl.CostEstimate(
+            flops=4 * grad.size * byte_cols, bytes_accessed=64 * grad.size, transcendentals=0
+        ),
+    )(grad, w, patch_rows, packed, gains)
 
 
 def norm_step(summed, gain_ref):
@@ -1312,14 +1370,19 @@
     grad_slots = grad_slots.reshape(count, byte_cols)
     grad_patch_out = owners(left_product(global_low, grad_slots))
     parts = right_product(grad_slots, w_patch_out).astype(BF).reshape(n_dp, patches, D)
-    grad_attend, grad_global_out, grad_mixer_low, alongs, grad_more, grad_patch_out = chain(
+    grad_attend, grad_more, grad_global_out, grad_mixer_low, alongs, grad_patch_out = chain(
         7,
-        [("sum", "dp", parts), ("sum1", "mp", grad_patch_out), ("sum", "mp", grad_attend)],
+        [
+            ("sum", "dp", parts),
+            ("sum1", "mp", grad_patch_out),
+            ("sum", "mp", grad_attend),
+            ("sum", "mp", grad_more),
+        ],
         grad_mixed_step,
         [unscaled],
         [row_low, lanes],
         [row],
-        [("agh", "dp", 0), ("agh", "dp", 1), ("sum", "mp", grad_more)],
+        [("agh", "dp", 0), ("agh", "dp", 1)],
         forwards=(1,),
     )
     grad_mixer_low = grad_mixer_low.reshape(count, D)
@@ -1399,16 +1462,10 @@
     grad_mixer_out = total(grad_mixer_out).reshape(-1)
     grad_attend, grad_more = total(grad_attend), total(grad_more)
     grad_global_low = grad_global_low.reshape(count, D)
-    grad_patch_rows = right_product(grad_global_low, w_patch_in).astype(BF)
-    grad_patch_in = left_product(patch_rows, grad_global_low).astype(BF)
-    grad_patch_rows, grad_patch_in, packed, gains = exchange(
-        11,
-        ("a2a", "dp", grad_patch_rows.reshape(n_dp, patches, byte_cols)),
-        ("sum", "mp", grad_patch_in.reshape(n_mp, -1, D)),
-        ("agh", "dp", total(packed)),
-        ("agh", "dp", total(gains)),
-    )
-    grad_patch_in = total(grad_patch_in).reshape(-1)
+    grad_patch_rows, grad_patch_in, packed, gains = patch_in_backward(
+        11, grad_global_low, w_patch_in, patch_rows, total(packed), total(gains), patches
+    )
+    grad_patch_in = grad_patch_in.reshape(-1)
     grad_patch_rows = grad_patch_rows.astype(F32).transpose(1, 0, 2).reshape(rows, D)
     grad_bytes = ((grad_local + grad_patch_rows) * keep).astype(BF)[None]
     out_bytes = ((after_attend + total(feed_parts)) * keep).astype(BF)[None]

time: 707 us -> 703 us (level)
    pallas_call x0 -> x1, Pallas kernels: none -> 43.5 us  [patch_in_backward(): pl.pallas_call(functools.partial(patch_in_kernel, sizes), out_shape=[jax....]
    pallas_call x2 -> x1, Pallas kernels: 91.2 us -> 50.8 us  [exchange(): pl.pallas_call(functools.partial(exchange_kernel, plan, sizes), out_shape...]
  transfers between devices with their start and end apart: 3 -> 3, of which waited for: 0 -> 0; matrix products, arithmetic and copies ran while one was open for 9% -> 8% of each run, Pallas kernels for 79% -> 80%
where the time goes in v2:
time: 703 us; the launch traced here: 698 us
  Pallas kernels  618 us (88%)
  local copies, waits for them, and re-layouts  30.1 us (4%)
  other arithmetic  24.5 us (3%)
  between operations  14.8 us (2%)
  matrix products  10.9 us (2%)
    pallas_call x4, Pallas kernels, chain(): pl.pallas_call(functools.partial(chain_kernel, tuple(((kind, axis) for ki...  342 us
    pallas_call x1, Pallas kernels, feed_section(): pl.pallas_call(functools.partial(feed_kernel, n_mp), out_shape=[jax.Shape...  61.7 us
    pallas_call x1, Pallas kernels, attend_backward(): pl.pallas_call(attend_backward_kernel, out_shape=[jax.ShapeDtypeStruct((r...  57.6 us
    pallas_call x1, Pallas kernels, exchange(): pl.pallas_call(functools.partial(exchange_kernel, plan, sizes), out_shape...  50.8 us
    pallas_call x1, Pallas kernels, attend_forward(): pl.pallas_call(attend_forward_kernel, out_shape=[jax.ShapeDtypeStruct((ro...  44.3 us
    pallas_call x1, Pallas kernels, patch_in_backward(): pl.pallas_call(functools.partial(patch_in_kernel, sizes), out_shape=[jax....  43.5 us
    pallas_call x2, Pallas kernels, whole_kernel(): pl.pallas_call(kernel, out_shape=shapes, in_specs=[vmem] * len(operands),...  17.8 us
  transfers between devices with their start and end apart: 3, of which 0 were waited for; matrix products, arithmetic and copies ran while one was open for 8% of the time, Pallas kernels for 80%

profile of v2, /device:TPU:0, one launch (start us, length us, event | category | flops | bytes accessed | tf_op | source)
XLA Modules:
  0.0 698.3 jit_solution(12261551999410226196)
XLA Ops:
  7.2 1.0 reshape.235
  8.3 0.9 reshape.236
  9.2 0.7 pad_maximum_fusion.2
  10.0 1.1 copy.92
  11.1 2.1 pad_maximum_fusion
  14.1 1.0 reshape.224.refs_2_
  15.3 1.1 copy.126
  16.4 0.7 reshape.227.refs_4_
  17.4 0.6 broadcast_in_dim_reshape.3.skip_ref
  18.1 1.3 dynamic_slice.23
  19.5 0.9 concatenate.24
  21.1 0.7 fusion.9
  22.0 2.3 fusion.7.refs_0_
  24.2 50.8 %shard_map.356 = (bf16[8,64,1024]{2,1,0:T(8,128)(2,1)}, bf16[8,32,896]{2,1,0:T(8,128)(2,1)}, bf16[4,256,1024]{2,1,0:T(8,128)(2,1)}) custom-call(bf16[8,64,1024]{2,1,0:T(8,128)(2,1)} %fusion.7.refs_0_, bf16[8,32,896]{2,1,0:T(8,128)(2,1)} %bitcast.134, bf16[256,1024]{1,0:T(8,128)(2,1)} %reshape.224.refs_2_), custom_call_target="tpu_custom_call" | custom-call | bytes 230686720 | tf_op jit(solution)/shard_map/pallas_call | solution.py:212
  75.0 4.6 fusion.17.refs_0_
  79.6 88.9 %shard_map.357 = (bf16[8,4,32,896]{3,2,1,0:T(8,128)(2,1)}, f32[64,1024]{1,0:T(8,128)}, bf16[8,64,1024]{2,1,0:T(8,128)(2,1)}, bf16[8,32,1024]{2,1,0:T(8,128)(2,1)}, bf16[4,64,1024]{2,1,0:T(8,128)(2,1)}) custom-call(f32[8,64,1024]{2,1,0:T(8,128)} %fusion.17.refs_0_, bf16[8,32,896]{2,1,0:T(8,128)(2,1)} %get-tuple-element.81.refs_1_, f32[1,1024]{1,0:T(1,128)} %bitcast.159, ...), custom_call_target="tpu_custom_call" | custom-call | bytes 96468992 | tf_op jit(solution)/shard_map/pallas_call | solution.py:336
  169.1 0.6 fusion.10
  170.9 6.2 shard_map.358
  177.1 1.7 fusion.1
  178.9 84.3 %shard_map.359 = (bf16[8,4,32,1024]{3,2,1,0:T(8,128)(2,1)}, bf16[4,512,1024]{2,1,0:T(8,128)(2,1)}, f32[64,1024]{1,0:T(8,128)}, bf16[8,64,1024]{2,1,0:T(8,128)(2,1)}, f32[8,64,128]{2,1,0:T(8,128)}) custom-call(bf16[8,64,1024]{2,1,0:T(8,128)(2,1)} %bitcast.136, f32[8,64,128]{2,1,0:T(8,128)} %bitcast.152, bf16[8,32,1024]{2,1,0:T(8,128)(2,1)} %get-tuple-element.87.refs_2_, ...), custom_call_target="tpu_custom_call" | custom-call | bytes 176160768 | tf_op jit(solution)/shard_map/pallas_call | solution.py:336
  263.2 44.3 %shard_map.360 = (f32[512,1024]{1,0:T(8,128)}, bf16[512,1024]{1,0:T(8,128)(2,1)}, bf16[512,3072]{1,0:T(8,128)(2,1)}, bf16[512,1024]{1,0:T(8,128)(2,1)}, f32[512,...) custom-call(bf16[512,1024]{1,0:T(8,128)(2,1)} %bitcast.183, bf16[1024,1024]{1,0:T(8,128)(2,1)} %bitcast.175, ...), custom_call_target="tpu_custom_call" | custom-call | flops 4294967296 | bytes 25165824 | tf_op jit(solution)/shard_map/pallas_call | solution.py:532
  307.5 61.7 %shard_map.361 = (bf16[2048,1024]{1,0:T(8,128)(2,1)}, f32[512,1024]{1,0:T(8,128)}, bf16[8,3,128,1024]{3,2,1,0:T(8,128)(2,1)}) custom-call(bf16[512,1024]{1,0:T(8,128)(2,1)} %get-tuple-element.92.x_ref, bf16[2048,1024]{1,0:T(8,128)(2,1)} %bitcast.172, bf16[8,3,128,1024]{3,2,1,0:T(8,128)(2,1)} %bitcast.171), custom_call_target="tpu_custom_call" | custom-call | flops 38654705664 | bytes 31457280 | tf_op jit(solution)/shard_map/pallas_call | solution.py:916
  369.3 57.6 %shard_map.362 = (f32[512,1024]{1,0:T(8,128)}, bf16[8,64,1024]{2,1,0:T(8,128)(2,1)}, bf16[4,8,32,2048]{3,2,1,0:T(8,128)(2,1)}, bf16[4,8,32,2048]{3,2,1,0:T(8,128...) custom-call(f32[512,1024]{1,0:T(8,128)} %get-tuple-element.94.grad_feed_ref, ...), custom_call_target="tpu_custom_call" | custom-call | flops 8589934592 | bytes 41943040 | tf_op jit(solution)/shard_map/pallas_call | solution.py:694
  426.9 3.7 convolution_convert_fusion
  430.7 2.6 bitcast_convert_fusion
  433.3 102.9 %shard_map.363 = (bf16[2,8,32,2048]{3,2,1,0:T(8,128)(2,1)}, bf16[2,8,32,2048]{3,2,1,0:T(8,128)(2,1)}, f32[64,1024]{1,0:T(8,128)}, bf16[8,64,1024]{2,1,0:T(8,128)...) custom-call(bf16[8,64,1024]{2,1,0:T(8,128)(2,1)} %bitcast.137, bf16[8,4,32,1024]{3,2,1,0:T(8,128)(2,1)} %bitcast.132, ...), custom_call_target="tpu_custom_call" | custom-call | bytes 738197504 | tf_op jit(solution)/shard_map/pallas_call | solution.py:336
  536.1 11.6 %shard_map.364 = (bf16[512,1024]{1,0:T(8,128)(2,1)}, bf16[1024,896]{1,0:T(8,128)(2,1)}, bf16[256,1024]{1,0:T(8,128)(2,1)}, f32[4,512]{1,0:T(4,128)}, f32[1,512]{...) custom-call(bf16[512,1024]{1,0:T(8,128)(2,1)} %bitcast.184, f32[512,128]{1,0:T(8,128)} %bitcast.187, ...), custom_call_target="tpu_custom_call" | custom-call | flops 2415919104 | bytes 32323584 | tf_op jit(solution)/shard_map/pallas_call | solution.py:1184
  547.8 0.9 slice_dynamic-update-slice_fusion
  549.2 1.3 reduce.5
  550.6 3.3 reduce_sum.124.refs_4_
  554.0 1.7 reduce_sum.126.refs_9_
  557.5 65.9 %shard_map.365 = (bf16[2,64,1024]{2,1,0:T(8,128)(2,1)}, bf16[2,512,1024]{2,1,0:T(8,128)(2,1)}, bf16[4,32,2048]{2,1,0:T(8,128)(2,1)}, f32[4,128,128]{2,1,0:T(8,12...) custom-call(bf16[8,64,1024]{2,1,0:T(8,128)(2,1)} %bitcast.135, ...), custom_call_target="tpu_custom_call" | custom-call | bytes 555745280 | tf_op jit(solution)/shard_map/pallas_call | solution.py:336
  623.4 1.2 convert_reduce_fusion.1
  624.6 1.1 convert_reduce_fusion.2
  625.8 0.8 copy.111
  627.1 1.3 reshape.259
  629.6 43.5 %shard_map.366 = (bf16[8,64,1024]{2,1,0:T(8,128)(2,1)}, f32[256,1024]{1,0:T(8,128)}, f32[8,128,128]{2,1,0:T(8,128)}, f32[8,8,1024]{2,1,0:T(8,128)}) custom-call(bf16[512,1024]{1,0:T(8,128)(2,1)} %bitcast.182, bf16[1024,1024]{1,0:T(8,128)(2,1)} %bitcast.174, bf16[512,1024]{1,0:T(8,128)(2,1)} %bitcast.179, f32[128,128]{1,0:T(8,128)} %reduce_sum.128.packed_ref, ...), custom_call_target="tpu_custom_call" | custom-call | flops 2147483648 | bytes 33554432 | tf_op jit(solution)/shard_map/pallas_call | solution.py:390
  673.2 2.5 copy.108
  676.4 0.7 slice.148
  677.7 0.7 copy.112
  678.4 0.8 copy.109
  679.9 1.2 copy.110
  682.1 0.7 fusion.14
  683.7 3.1 fusion.8
  686.8 1.5 copy.103
  688.5 0.8 slice_bitcast_fusion
  689.3 1.0 copy.100
  690.3 1.0 copy.101
  (143 shorter events, 12.6 us)
Async XLA Ops:
  7.2 6.1 copy-start.12
  7.2 256.0 %all-gather.4.cloned.1.call-start = ((), (), s32[]{:S(2)}) async-start(), calls=%async_computation.1 | async-start | bytes 8650752 | tf_op jit(solution)/shard_map/all_gather | solution.py:1245
  9.9 4.2 copy-start.8
  9.9 297.6 %all-gather.6.cloned.1.call-start = ((), (), s32[]{:S(2)}) async-start(), calls=%async_computation.2 | async-start | bytes 7077888 | tf_op jit(solution)/shard_map/all_gather | solution.py:1251
  11.1 4.0 copy-start.9
  13.2 3.2 copy-start.17
  13.2 3.9 copy-start.24
  13.2 4.0 copy-start.25
  13.2 4.0 copy-start.26
  13.2 4.8 slice-start.2
  13.3 673.5 %reduce-scatter.4.cloned.1.call-start = ((), (), s32[]{:S(2)}) async-start(), calls=%async_computation.3 | async-start | bytes 7077888
  15.1 5.4 copy-start.27
  15.1 6.6 copy-start
  79.6 90.1 %slice-start.3 = ((f32[2304]{0:T(1024)}), f32[256]{0:T(256)S(1)}, s32[]{:S(2)}) async-start(f32[2304]{0:T(1024)} %param.34), calls=%async_computation.7 | async-start | bytes 2048 | tf_op jit(solution)/shard_map/slice | solution.py:1294
  79.6 90.7 %slice-start = ((f32[4,2304]{1,0:T(4,128)}), f32[4,2048]{1,0:T(4,128)S(1)}, s32[]{:S(2)}) async-start(f32[4,2304]{1,0:T(4,128)} %param.33), calls=%async_computation.4 | async-start | bytes 65536 | tf_op jit(solution)/shard_map/slice | solution.py:1294
  79.6 90.7 %slice-start.1 = ((f32[4,2304]{1,0:T(4,128)}), f32[4,256]{1,0:T(4,128)S(1)}, s32[]{:S(2)}) async-start(f32[4,2304]{1,0:T(4,128)} %param.33), calls=%async_computation.5 | async-start | bytes 8192 | tf_op jit(solution)/shard_map/slice | solution.py:1294
  170.9 6.2 copy-start.6
  369.2 57.7 %copy-start.22 = (bf16[8,4,32,1024]{3,2,1,0:T(8,128)(2,1)S(1)}, bf16[8,4,32,1024]{3,2,1,0:T(8,128)(2,1)}, u32[]{:S(2)}) copy-start(bf16[8,4,32,1024]{3,2,1,0:T(8,128)(2,1)} %get-tuple-element.90) | copy-start | bytes 6291460
  426.9 3.7 copy-start.23
  426.9 3.7 copy-start.28
  547.8 6.2 copy-start.2
  554.0 1.7 copy-start.20
  554.0 2.0 copy-start.21
  554.0 2.6 copy-start.29
  554.0 2.8 copy-start.18
  554.0 2.8 copy-start.19
  623.4 3.2 copy-start.11
  626.8 1.6 copy-start.13
  626.8 2.2 copy-start.16
  673.1 2.5 copy-start.10
  673.1 3.9 copy-start.14
  673.2 5.2 copy-start.15
  673.2 6.0 copy-start.7
  679.2 1.8 copy-start.1
  681.0 2.3 copy-start.5
  681.0 2.6 copy-start.4
  681.5 2.2 copy-start.3
Sparse Core Ops, SparseCore 0:
  11.5 120.0 all-gather.3
  134.3 139.7 all-gather.5
  369.4 163.1 reduce-scatter.3
